TPU v7x, 512 devices: a whole 4x8x8 slice. The times are simulated.
512 devices in a mesh: shot: 8 (over x, z_hi), dom: 64 (over y, z_lo, core).
Axes of the slice: x: 4, y: 8, z: 8 (z_hi: 2, z_lo: 4; z = z_hi * 4 + z_lo), core: 2. Of those that a mesh axis runs over, the one named last changes fastest.
Arguments:
- source_prev: float32 [8, 256, 64, 128], P('shot', 'dom'), may hold values from -6 to 6
- source_now: float32 [8, 256, 64, 128], P('shot', 'dom'), may hold values from -6 to 6
- adjoint_prev: float32 [8, 256, 64, 128], P('shot', 'dom'), may hold values from -6 to 6
- adjoint_now: float32 [8, 256, 64, 128], P('shot', 'dom'), may hold values from -6 to 6
- squared_courant: float32 [256, 64, 256], P('dom', 'shot'), may hold values from 0.03 to 0.15
- offsets: int32 [8], P('shot'), may hold values from 0 to 128, as said below
- traces: float32 [8, 8, 8192], P('shot', None, 'dom'), may hold values from -6 to 6
- receiver_cells: int32 [8, 1, 8192], P('shot', None, 'dom'), may hold values from 0 to 32767
- counts: int32 [8, 64, 64], P('shot', 'dom'), may hold values from 0 to 2, as said below
Outputs:
- source_field: float32 [8, 256, 64, 128], P('shot', 'dom')
- adjoint_field: float32 [8, 256, 64, 128], P('shot', 'dom')
- gradient: float32 [256, 64, 256], P('dom', 'shot')
Inputs may be any that keep to these rules, and one draw needn't show every extreme that they name: `counts`: in every shot, some source device fills all 2 slots for some owner. The shots' offsets are distinct, and one of them is exactly 128.
All inputs are finite; a program needn't handle non-finite values.
Results may differ from a plain program's by a relative error of at most 0.0003.
Values sent between devices are 32-bit elements; how exact they have to be, the bound alone decides.
A program may use at most 64 MiB of HBM per device.

v0:
```python
import jax
import jax.numpy as jnp
from jax import lax
from jax.sharding import PartitionSpec as P

NZ = 128
STEPS = 8
CAP = 2
NZM = 256


COEFFS = (-205.0 / 72.0, 8.0 / 5.0, -1.0 / 5.0, 8.0 / 315.0, -1.0 / 560.0)


def padded_2(block, sides, width):
    for axis, dim in sides:
        count = lax.axis_size(axis)
        forward = [(i, i + 1) for i in range(count - 1)]
        backward = [(target, source) for source, target in forward]
        low = lax.ppermute(
            lax.slice_in_dim(block, block.shape[dim] - width, None, axis=dim), axis, forward
        )
        high = lax.ppermute(lax.slice_in_dim(block, 0, width, axis=dim), axis, backward)
        block = jnp.concatenate([low, block, high], axis=dim)
    return block


def laplace(padded):
    size_x = padded.shape[0] - 8
    size_y = padded.shape[1] - 8
    size_z = padded.shape[2] - 8
    center = padded[4 : 4 + size_x, 4 : 4 + size_y, 4 : 4 + size_z]
    total = 3.0 * COEFFS[0] * center
    for reach in range(1, 5):
        pair = (
            padded[4 + reach : 4 + reach + size_x, 4 : 4 + size_y, 4 : 4 + size_z]
            + padded[4 - reach : 4 - reach + size_x, 4 : 4 + size_y, 4 : 4 + size_z]
        )
        pair = (
            pair
            + padded[4 : 4 + size_x, 4 + reach : 4 + reach + size_y, 4 : 4 + size_z]
            + padded[4 : 4 + size_x, 4 - reach : 4 - reach + size_y, 4 : 4 + size_z]
        )
        pair = (
            pair
            + padded[4 : 4 + size_x, 4 : 4 + size_y, 4 + reach : 4 + reach + size_z]
            + padded[4 : 4 + size_x, 4 : 4 + size_y, 4 - reach : 4 - reach + size_z]
        )
        total = total + COEFFS[reach] * pair
    return total


def side_pad(extended):
    return jnp.pad(extended, ((0, 0), (4, 4), (4, 4)))


def shards(
    source_prev,
    source_now,
    adjoint_prev,
    adjoint_now,
    squared_courant,
    offsets,
    traces,
    receiver_cells,
    counts,
):
    src_prev = source_prev[0]
    src_now = source_now[0]
    adj_prev = adjoint_prev[0]
    adj_now = adjoint_now[0]
    offset = offsets[0]
    whole_rows = lax.all_gather(squared_courant, "shot", axis=1, tiled=True)
    courant = lax.dynamic_slice_in_dim(whole_rows, offset, NZ, 2)
    live = jnp.arange(CAP, dtype=jnp.int32)[None, :] < counts[0, 0][:, None]
    masked = jnp.where(live.reshape(1, 1, -1), traces, jnp.float32(0.0))
    arrived, arrived_cells = (
        lax.all_to_all(masked, "dom", split_axis=2, concat_axis=2, tiled=True),
        lax.all_to_all(receiver_cells, "dom", split_axis=2, concat_axis=2, tiled=True),
    )
    index = arrived_cells[0, 0]
    image = jnp.zeros(src_now.shape, jnp.float32)
    for moment in range(STEPS):
        lap_source = laplace(side_pad(padded_2(src_now, (("dom", 0),), 4)))
        lap_adjoint = laplace(side_pad(padded_2(adj_now, (("dom", 0),), 4)))
        image = image + adj_now * lap_source
        src_next = 2.0 * src_now - src_prev + courant * lap_source
        adj_next = 2.0 * adj_now - adj_prev + courant * lap_adjoint
        adj_next = adj_next.reshape(-1).at[index].add(arrived[0, moment]).reshape(adj_now.shape)
        src_prev, src_now = (src_now, src_next)
        adj_prev, adj_now = (adj_now, adj_next)
    placed = lax.dynamic_update_slice(
        jnp.zeros((src_now.shape[0], src_now.shape[1], NZM), jnp.float32),
        image / STEPS,
        (jnp.int32(0), jnp.int32(0), offset),
    )
    total = lax.psum(placed, "shot")
    tile_rows = squared_courant.shape[1]
    gradient = lax.dynamic_slice_in_dim(total, lax.axis_index("shot") * tile_rows, tile_rows, 1)
    return (src_now[None], adj_now[None], gradient)


def solution(mesh):
    placed = (
        P("shot", "dom", None, None),
        P("shot", "dom", None, None),
        P("shot", "dom", None, None),
        P("shot", "dom", None, None),
        P("dom", "shot", None),
        P("shot"),
        P("shot", None, "dom"),
        P("shot", None, "dom"),
        P("shot", "dom", None),
    )
    return jax.shard_map(
        shards,
        mesh=mesh,
        in_specs=placed,
        out_specs=(
            P("shot", "dom", None, None),
            P("shot", "dom", None, None),
            P("dom", "shot", None),
        ),
        check_vma=False,
    )
```

profile of v0, /device:TPU:16, one launch (start us, length us, event | category | flops | bytes accessed | tf_op | source)
XLA Modules:
  0.0 350.0 jit_solution(15722235077917498028)
XLA Ops:
  7.2 1.9 collective-permute-start.17
  9.1 7.2 %collective-permute-start.16 = (f32[4,64,128]{2,1,0:T(8,128)}, f32[4,64,128]{2,1,0:T(8,128)S(1)}, u32[]{:S(2)}, u32[]{:S(2)}) collective-permute-start(f32[4,64,128]{2,1,0:T(8,128)} %bitcast.92), channel_id=1, source_target_pairs={{1,0},{2,1},{3,2},{4,3},{5,4},{6,5},{7,6},{8,7},{9,8},{10,9},{11,1... | collective-permute-start | bytes 393224 | tf_op jit(solution)/shard_map/ppermute | solution.py:23
  16.3 2.6 collective-permute-start
  18.9 1.9 collective-permute-start.1
  20.9 0.7 copy.20
  21.6 12.1 %all-to-all-start = ((s32[1,1,128]{1,0,2:T(1,128)}), s32[1,1,128]{1,0,2:T(1,128)S(1)}, u32[]{:S(2)}, u32[]{:S(2)}) async-start(s32[1,1,128]{1,0,2:T(1,128)} %copy.20), calls=%async_computation | async-start | bytes 131072 | tf_op jit(solution)/shard_map/all_to_all | solution.py:79
  33.7 46.4 %all_gather.3 = f32[4,64,256]{2,1,0:T(8,128)S(1)} all-gather(f32[4,8,256]{2,1,0:T(8,128)S(1)} %copy-done.6), channel_id=1, replica_groups=mesh['shot'=8,'dom'=64] {'shot'}, dimensions={1}, use_global_device_ids=true | all-gather | bytes 294912 | tf_op jit(solution)/shard_map/all_gather | solution.py:73
  80.8 0.6 copy-done.9
  82.2 0.7 copy.21
  83.0 10.7 %all-to-all-start.1 = ((f32[1,8,128]{1,0,2:T(1,128)}), f32[1,8,128]{1,0,2:T(1,128)S(1)}, u32[]{:S(2)}, u32[]{:S(2)}) async-start(f32[1,8,128]{1,0,2:T(1,128)} %copy.21), calls=%async_computation.1 | async-start | bytes 131072 | tf_op jit(solution)/shard_map/all_to_all | solution.py:78
  93.8 2.4 reduce
  96.1 5.9 %all-to-all-done.1 = f32[1,8,128]{1,0,2:T(1,128)S(1)} async-done(((f32[1,8,128]{1,0,2:T(1,128)}), f32[1,8,128]{1,0,2:T(1,128)S(1)}, u32[]{:S(2)}, u32[]{:S(2)}) %all-to-all-start.1) | async-done | bytes 4128 | tf_op jit(solution)/shard_map/all_to_all | solution.py:78
  102.1 3.2 slice_reduce_fusion
  106.8 3.3 collective-permute-start.2
  110.0 1.9 collective-permute-start.3
  112.3 0.6 fusion.168
  112.9 1.3 scatter_fusion
  114.3 2.5 collective-permute-start.19
  116.8 5.7 %collective-permute-start.18 = (f32[4,64,128]{2,1,0:T(8,128)S(1)}, f32[4,64,128]{2,1,0:T(8,128)S(1)}, u32[]{:S(2)}, u32[]{:S(2)}) collective-permute-start(f32[4,64,128]{2,1,0:T(8,128)S(1)} %bitcast.43), channel_id=1, source_target_pairs={{1,0},{2,1},{3,2},{4,3},{5,4},{6,5},{7,6},{8,7},{9,8},{10,9},{11,1... | collective-permute-start | bytes 393224 | tf_op jit(solution)/shard_map/ppermute | solution.py:23
  122.9 0.6 multiply_add_fusion.5
  123.5 2.4 collective-permute-start.4
  125.9 1.9 collective-permute-start.5
  128.2 0.6 fusion.146
  128.8 1.5 scatter_fusion.1
  130.3 1.9 collective-permute-start.21
  132.3 6.3 %collective-permute-start.20 = (f32[4,64,128]{2,1,0:T(8,128)S(1)}, f32[4,64,128]{2,1,0:T(8,128)S(1)}, u32[]{:S(2)}, u32[]{:S(2)}) collective-permute-start(f32[4,64,128]{2,1,0:T(8,128)S(1)} %bitcast.50), channel_id=1, source_target_pairs={{1,0},{2,1},{3,2},{4,3},{5,4},{6,5},{7,6},{8,7},{9,8},{10,9},{11,1... | collective-permute-start | bytes 393224 | tf_op jit(solution)/shard_map/ppermute | solution.py:23
  138.9 0.6 multiply_add_fusion.4
  139.5 2.4 collective-permute-start.6
  142.0 1.9 collective-permute-start.7
  144.8 1.3 scatter_fusion.2
  146.2 1.9 collective-permute-start.23
  148.1 6.3 %collective-permute-start.22 = (f32[4,64,128]{2,1,0:T(8,128)S(1)}, f32[4,64,128]{2,1,0:T(8,128)S(1)}, u32[]{:S(2)}, u32[]{:S(2)}) collective-permute-start(f32[4,64,128]{2,1,0:T(8,128)S(1)} %bitcast.57), channel_id=1, source_target_pairs={{1,0},{2,1},{3,2},{4,3},{5,4},{6,5},{7,6},{8,7},{9,8},{10,9},{11,1... | collective-permute-start | bytes 393224 | tf_op jit(solution)/shard_map/ppermute | solution.py:23
  154.8 0.6 multiply_add_fusion.3
  155.4 2.4 collective-permute-start.8
  157.8 1.9 collective-permute-start.9
  160.7 1.3 scatter_fusion.3
  162.0 1.9 collective-permute-start.25
  164.0 6.3 %collective-permute-start.24 = (f32[4,64,128]{2,1,0:T(8,128)S(1)}, f32[4,64,128]{2,1,0:T(8,128)S(1)}, u32[]{:S(2)}, u32[]{:S(2)}) collective-permute-start(f32[4,64,128]{2,1,0:T(8,128)S(1)} %bitcast.64), channel_id=1, source_target_pairs={{1,0},{2,1},{3,2},{4,3},{5,4},{6,5},{7,6},{8,7},{9,8},{10,9},{11,1... | collective-permute-start | bytes 393224 | tf_op jit(solution)/shard_map/ppermute | solution.py:23
  170.6 0.6 multiply_add_fusion.2
  171.3 2.4 collective-permute-start.10
  173.7 1.9 collective-permute-start.11
  175.9 0.6 fusion.80
  176.6 1.3 scatter_fusion.4
  177.9 1.9 collective-permute-start.27
  179.8 6.3 %collective-permute-start.26 = (f32[4,64,128]{2,1,0:T(8,128)S(1)}, f32[4,64,128]{2,1,0:T(8,128)S(1)}, u32[]{:S(2)}, u32[]{:S(2)}) collective-permute-start(f32[4,64,128]{2,1,0:T(8,128)S(1)} %bitcast.71), channel_id=1, source_target_pairs={{1,0},{2,1},{3,2},{4,3},{5,4},{6,5},{7,6},{8,7},{9,8},{10,9},{11,1... | collective-permute-start | bytes 393224 | tf_op jit(solution)/shard_map/ppermute | solution.py:23
  186.5 0.6 multiply_add_fusion.1
  187.1 2.4 collective-permute-start.12
  189.5 1.9 collective-permute-start.13
  192.4 1.3 scatter_fusion.5
  193.8 2.1 collective-permute-start.29
  195.9 6.3 %collective-permute-start.28 = (f32[4,64,128]{2,1,0:T(8,128)S(1)}, f32[4,64,128]{2,1,0:T(8,128)S(1)}, u32[]{:S(2)}, u32[]{:S(2)}) collective-permute-start(f32[4,64,128]{2,1,0:T(8,128)S(1)} %bitcast.78), channel_id=1, source_target_pairs={{1,0},{2,1},{3,2},{4,3},{5,4},{6,5},{7,6},{8,7},{9,8},{10,9},{11,1... | collective-permute-start | bytes 393224 | tf_op jit(solution)/shard_map/ppermute | solution.py:23
  202.6 0.6 multiply_add_fusion
  203.2 2.4 collective-permute-start.14
  205.6 1.9 collective-permute-start.15
  208.5 1.3 scatter_fusion.6
  209.8 1.9 collective-permute-start.31
  211.8 6.3 %collective-permute-start.30 = (f32[4,64,128]{2,1,0:T(8,128)S(1)}, f32[4,64,128]{2,1,0:T(8,128)S(1)}, u32[]{:S(2)}, u32[]{:S(2)}) collective-permute-start(f32[4,64,128]{2,1,0:T(8,128)S(1)} %bitcast.85), channel_id=1, source_target_pairs={{1,0},{2,1},{3,2},{4,3},{5,4},{6,5},{7,6},{8,7},{9,8},{10,9},{11,1... | collective-permute-start | bytes 393224 | tf_op jit(solution)/shard_map/ppermute | solution.py:23
  219.1 1.1 dynamic_update_slice.3
  220.2 0.7 copy-done.3
  221.2 0.6 fusion.14
  221.9 1.3 scatter_fusion.7
  223.2 0.8 add_bitcast_fusion
  224.0 117.8 %all-reduce.18.cloned.1.call-done = f32[4,64,256]{2,1,0:T(8,128)} async-done(((f32[4,64,256]{2,1,0:T(8,128)}), f32[4,64,256]{2,1,0:T(8,128)}) %all-reduce.18.cloned.1.call-update) | async-done | bytes 262160 | tf_op jit(solution)/shard_map/psum | solution.py:97
  341.8 1.4 constant_dynamic-slice_fusion
  (80 shorter events, 10.0 us)
Async XLA Ops:
  7.2 13.7 %copy-start.8 = (s32[1,1,128]{2,1,0:T(1,128)S(1)}, s32[1,1,128]{2,1,0:T(1,128)}, u32[]{:S(2)}) copy-start(s32[1,1,128]{2,1,0:T(1,128)} %param.16) | copy-start | bytes 1540
  7.2 104.8 %collective-permute-start.17 = (f32[4,64,128]{2,1,0:T(8,128)}, f32[4,64,128]{2,1,0:T(8,128)S(1)}, u32[]{:S(2)}, u32[]{:S(2)}) collective-permute-start(f32[4,64,128]{2,1,0:T(8,128)} %bitcast.91), channel_id=1, source_target_pairs={{0,1},{1,2},{2,3},{3,4},{4,5},{5,6},{6,7},{7,8},{8,9},{9,10},{10,1... | collective-permute-start | bytes 393224 | tf_op jit(solution)/shard_map/ppermute | solution.py:20
  9.1 102.9 %collective-permute-start.16 = (f32[4,64,128]{2,1,0:T(8,128)}, f32[4,64,128]{2,1,0:T(8,128)S(1)}, u32[]{:S(2)}, u32[]{:S(2)}) collective-permute-start(f32[4,64,128]{2,1,0:T(8,128)} %bitcast.92), channel_id=1, source_target_pairs={{1,0},{2,1},{3,2},{4,3},{5,4},{6,5},{7,6},{8,7},{9,8},{10,9},{11,1... | collective-permute-start | bytes 393224 | tf_op jit(solution)/shard_map/ppermute | solution.py:23
  16.3 88.9 %collective-permute-start = (f32[4,64,128]{2,1,0:T(8,128)}, f32[4,64,128]{2,1,0:T(8,128)S(1)}, u32[]{:S(2)}, u32[]{:S(2)}) collective-permute-start(f32[4,64,128]{2,1,0:T(8,128)} %bitcast.95), channel_id=1, source_target_pairs={{1,0},{2,1},{3,2},{4,3},{5,4},{6,5},{7,6},{8,7},{9,8},{10,9},{11,1... | collective-permute-start | bytes 393224 | tf_op jit(solution)/shard_map/ppermute | solution.py:23
  18.9 86.3 %collective-permute-start.1 = (f32[4,64,128]{2,1,0:T(8,128)}, f32[4,64,128]{2,1,0:T(8,128)S(1)}, u32[]{:S(2)}, u32[]{:S(2)}) collective-permute-start(f32[4,64,128]{2,1,0:T(8,128)} %bitcast.96), channel_id=1, source_target_pairs={{0,1},{1,2},{2,3},{3,4},{4,5},{5,6},{6,7},{7,8},{8,9},{9,10},{10,1... | collective-permute-start | bytes 393224 | tf_op jit(solution)/shard_map/ppermute | solution.py:20
  21.6 12.1 %copy-start.6 = (f32[4,8,256]{2,1,0:T(8,128)S(1)}, f32[4,8,256]{2,1,0:T(8,128)}, u32[]{:S(2)}) copy-start(f32[4,8,256]{2,1,0:T(8,128)} %param.13) | copy-start | bytes 98308
  21.6 61.4 %all-to-all-start = ((s32[1,1,128]{1,0,2:T(1,128)}), s32[1,1,128]{1,0,2:T(1,128)S(1)}, u32[]{:S(2)}, u32[]{:S(2)}) async-start(s32[1,1,128]{1,0,2:T(1,128)} %copy.20), calls=%async_computation | async-start | bytes 131072 | tf_op jit(solution)/shard_map/all_to_all | solution.py:79
  80.8 0.7 copy-start.9
  81.5 0.7 copy-start.7
  83.0 19.1 %all-to-all-start.1 = ((f32[1,8,128]{1,0,2:T(1,128)}), f32[1,8,128]{1,0,2:T(1,128)S(1)}, u32[]{:S(2)}, u32[]{:S(2)}) async-start(f32[1,8,128]{1,0,2:T(1,128)} %copy.21), calls=%async_computation.1 | async-start | bytes 131072 | tf_op jit(solution)/shard_map/all_to_all | solution.py:78
  93.7 248.1 %all-reduce.18.cloned.1.call-start = ((), (), s32[]{:S(2)}) async-start(), calls=%async_computation.2 | async-start | bytes 524288 | tf_op jit(solution)/shard_map/psum | solution.py:97
  96.1 9.2 %copy-start.2 = (f32[1,4,64,128]{3,2,1,0:T(8,128)S(1)}, f32[1,4,64,128]{3,2,1,0:T(8,128)}, u32[]{:S(2)}) copy-start(f32[1,4,64,128]{3,2,1,0:T(8,128)} %param.10) | copy-start | bytes 393220
  105.2 0.9 copy-start.5
  106.1 5.9 %copy-start.1 = (f32[1,4,64,128]{3,2,1,0:T(8,128)S(1)}, f32[1,4,64,128]{3,2,1,0:T(8,128)}, u32[]{:S(2)}) copy-start(f32[1,4,64,128]{3,2,1,0:T(8,128)} %param.12) | copy-start | bytes 393220
  106.8 5.5 %copy-start.4 = (f32[1,4,64,128]{3,2,1,0:T(8,128)S(1)}, f32[1,4,64,128]{3,2,1,0:T(8,128)}, u32[]{:S(2)}) copy-start(f32[1,4,64,128]{3,2,1,0:T(8,128)} %param.11) | copy-start | bytes 393220
  106.8 15.8 %collective-permute-start.2 = (f32[4,64,128]{2,1,0:T(8,128)S(1)}, f32[4,64,128]{2,1,0:T(8,128)S(1)}, u32[]{:S(2)}, u32[]{:S(2)}) collective-permute-start(f32[4,64,128]{2,1,0:T(8,128)S(1)} %get-tuple-element.25), channel_id=1, source_target_pairs={{1,0},{2,1},{3,2},{4,3},{5,4},{6,5},{7,6},{8,7},{9,8},{10,9},{11,1... | collective-permute-start | bytes 393224 | tf_op jit(solution)/shard_map/ppermute | solution.py:23
  110.0 12.5 %collective-permute-start.3 = (f32[4,64,128]{2,1,0:T(8,128)S(1)}, f32[4,64,128]{2,1,0:T(8,128)S(1)}, u32[]{:S(2)}, u32[]{:S(2)}) collective-permute-start(f32[4,64,128]{2,1,0:T(8,128)S(1)} %get-tuple-element.25), channel_id=1, source_target_pairs={{0,1},{1,2},{2,3},{3,4},{4,5},{5,6},{6,7},{7,8},{8,9},{9,10},{10,1... | collective-permute-start | bytes 393224 | tf_op jit(solution)/shard_map/ppermute | solution.py:20
  114.3 13.6 %collective-permute-start.19 = (f32[4,64,128]{2,1,0:T(8,128)S(1)}, f32[4,64,128]{2,1,0:T(8,128)S(1)}, u32[]{:S(2)}, u32[]{:S(2)}) collective-permute-start(f32[4,64,128]{2,1,0:T(8,128)S(1)} %bitcast.42), channel_id=1, source_target_pairs={{0,1},{1,2},{2,3},{3,4},{4,5},{5,6},{6,7},{7,8},{8,9},{9,10},{10,1... | collective-permute-start | bytes 393224 | tf_op jit(solution)/shard_map/ppermute | solution.py:20
  116.8 11.0 %collective-permute-start.18 = (f32[4,64,128]{2,1,0:T(8,128)S(1)}, f32[4,64,128]{2,1,0:T(8,128)S(1)}, u32[]{:S(2)}, u32[]{:S(2)}) collective-permute-start(f32[4,64,128]{2,1,0:T(8,128)S(1)} %bitcast.43), channel_id=1, source_target_pairs={{1,0},{2,1},{3,2},{4,3},{5,4},{6,5},{7,6},{8,7},{9,8},{10,9},{11,1... | collective-permute-start | bytes 393224 | tf_op jit(solution)/shard_map/ppermute | solution.py:23
  123.5 15.1 %collective-permute-start.4 = (f32[4,64,128]{2,1,0:T(8,128)S(1)}, f32[4,64,128]{2,1,0:T(8,128)S(1)}, u32[]{:S(2)}, u32[]{:S(2)}) collective-permute-start(f32[4,64,128]{2,1,0:T(8,128)S(1)} %get-tuple-element.23), channel_id=1, source_target_pairs={{1,0},{2,1},{3,2},{4,3},{5,4},{6,5},{7,6},{8,7},{9,8},{10,9},{11,1... | collective-permute-start | bytes 393224 | tf_op jit(solution)/shard_map/ppermute | solution.py:23
  125.9 12.7 %collective-permute-start.5 = (f32[4,64,128]{2,1,0:T(8,128)S(1)}, f32[4,64,128]{2,1,0:T(8,128)S(1)}, u32[]{:S(2)}, u32[]{:S(2)}) collective-permute-start(f32[4,64,128]{2,1,0:T(8,128)S(1)} %get-tuple-element.23), channel_id=1, source_target_pairs={{0,1},{1,2},{2,3},{3,4},{4,5},{5,6},{6,7},{7,8},{8,9},{9,10},{10,1... | collective-permute-start | bytes 393224 | tf_op jit(solution)/shard_map/ppermute | solution.py:20
  130.3 13.6 %collective-permute-start.21 = (f32[4,64,128]{2,1,0:T(8,128)S(1)}, f32[4,64,128]{2,1,0:T(8,128)S(1)}, u32[]{:S(2)}, u32[]{:S(2)}) collective-permute-start(f32[4,64,128]{2,1,0:T(8,128)S(1)} %bitcast.49), channel_id=1, source_target_pairs={{0,1},{1,2},{2,3},{3,4},{4,5},{5,6},{6,7},{7,8},{8,9},{9,10},{10,1... | collective-permute-start | bytes 393224 | tf_op jit(solution)/shard_map/ppermute | solution.py:20
  132.3 11.7 %collective-permute-start.20 = (f32[4,64,128]{2,1,0:T(8,128)S(1)}, f32[4,64,128]{2,1,0:T(8,128)S(1)}, u32[]{:S(2)}, u32[]{:S(2)}) collective-permute-start(f32[4,64,128]{2,1,0:T(8,128)S(1)} %bitcast.50), channel_id=1, source_target_pairs={{1,0},{2,1},{3,2},{4,3},{5,4},{6,5},{7,6},{8,7},{9,8},{10,9},{11,1... | collective-permute-start | bytes 393224 | tf_op jit(solution)/shard_map/ppermute | solution.py:23
  139.5 14.9 %collective-permute-start.6 = (f32[4,64,128]{2,1,0:T(8,128)S(1)}, f32[4,64,128]{2,1,0:T(8,128)S(1)}, u32[]{:S(2)}, u32[]{:S(2)}) collective-permute-start(f32[4,64,128]{2,1,0:T(8,128)S(1)} %get-tuple-element.21), channel_id=1, source_target_pairs={{1,0},{2,1},{3,2},{4,3},{5,4},{6,5},{7,6},{8,7},{9,8},{10,9},{11,1... | collective-permute-start | bytes 393224 | tf_op jit(solution)/shard_map/ppermute | solution.py:23
  142.0 12.5 %collective-permute-start.7 = (f32[4,64,128]{2,1,0:T(8,128)S(1)}, f32[4,64,128]{2,1,0:T(8,128)S(1)}, u32[]{:S(2)}, u32[]{:S(2)}) collective-permute-start(f32[4,64,128]{2,1,0:T(8,128)S(1)} %get-tuple-element.21), channel_id=1, source_target_pairs={{0,1},{1,2},{2,3},{3,4},{4,5},{5,6},{6,7},{7,8},{8,9},{9,10},{10,1... | collective-permute-start | bytes 393224 | tf_op jit(solution)/shard_map/ppermute | solution.py:20
  146.2 13.6 %collective-permute-start.23 = (f32[4,64,128]{2,1,0:T(8,128)S(1)}, f32[4,64,128]{2,1,0:T(8,128)S(1)}, u32[]{:S(2)}, u32[]{:S(2)}) collective-permute-start(f32[4,64,128]{2,1,0:T(8,128)S(1)} %bitcast.56), channel_id=1, source_target_pairs={{0,1},{1,2},{2,3},{3,4},{4,5},{5,6},{6,7},{7,8},{8,9},{9,10},{10,1... | collective-permute-start | bytes 393224 | tf_op jit(solution)/shard_map/ppermute | solution.py:20
  148.1 11.7 %collective-permute-start.22 = (f32[4,64,128]{2,1,0:T(8,128)S(1)}, f32[4,64,128]{2,1,0:T(8,128)S(1)}, u32[]{:S(2)}, u32[]{:S(2)}) collective-permute-start(f32[4,64,128]{2,1,0:T(8,128)S(1)} %bitcast.57), channel_id=1, source_target_pairs={{1,0},{2,1},{3,2},{4,3},{5,4},{6,5},{7,6},{8,7},{9,8},{10,9},{11,1... | collective-permute-start | bytes 393224 | tf_op jit(solution)/shard_map/ppermute | solution.py:23
  155.4 14.9 %collective-permute-start.8 = (f32[4,64,128]{2,1,0:T(8,128)S(1)}, f32[4,64,128]{2,1,0:T(8,128)S(1)}, u32[]{:S(2)}, u32[]{:S(2)}) collective-permute-start(f32[4,64,128]{2,1,0:T(8,128)S(1)} %get-tuple-element.19), channel_id=1, source_target_pairs={{1,0},{2,1},{3,2},{4,3},{5,4},{6,5},{7,6},{8,7},{9,8},{10,9},{11,1... | collective-permute-start | bytes 393224 | tf_op jit(solution)/shard_map/ppermute | solution.py:23
  157.8 12.5 %collective-permute-start.9 = (f32[4,64,128]{2,1,0:T(8,128)S(1)}, f32[4,64,128]{2,1,0:T(8,128)S(1)}, u32[]{:S(2)}, u32[]{:S(2)}) collective-permute-start(f32[4,64,128]{2,1,0:T(8,128)S(1)} %get-tuple-element.19), channel_id=1, source_target_pairs={{0,1},{1,2},{2,3},{3,4},{4,5},{5,6},{6,7},{7,8},{8,9},{9,10},{10,1... | collective-permute-start | bytes 393224 | tf_op jit(solution)/shard_map/ppermute | solution.py:20
  162.0 13.6 %collective-permute-start.25 = (f32[4,64,128]{2,1,0:T(8,128)S(1)}, f32[4,64,128]{2,1,0:T(8,128)S(1)}, u32[]{:S(2)}, u32[]{:S(2)}) collective-permute-start(f32[4,64,128]{2,1,0:T(8,128)S(1)} %bitcast.63), channel_id=1, source_target_pairs={{0,1},{1,2},{2,3},{3,4},{4,5},{5,6},{6,7},{7,8},{8,9},{9,10},{10,1... | collective-permute-start | bytes 393224 | tf_op jit(solution)/shard_map/ppermute | solution.py:20
  164.0 11.7 %collective-permute-start.24 = (f32[4,64,128]{2,1,0:T(8,128)S(1)}, f32[4,64,128]{2,1,0:T(8,128)S(1)}, u32[]{:S(2)}, u32[]{:S(2)}) collective-permute-start(f32[4,64,128]{2,1,0:T(8,128)S(1)} %bitcast.64), channel_id=1, source_target_pairs={{1,0},{2,1},{3,2},{4,3},{5,4},{6,5},{7,6},{8,7},{9,8},{10,9},{11,1... | collective-permute-start | bytes 393224 | tf_op jit(solution)/shard_map/ppermute | solution.py:23
  171.3 14.9 %collective-permute-start.10 = (f32[4,64,128]{2,1,0:T(8,128)S(1)}, f32[4,64,128]{2,1,0:T(8,128)S(1)}, u32[]{:S(2)}, u32[]{:S(2)}) collective-permute-start(f32[4,64,128]{2,1,0:T(8,128)S(1)} %get-tuple-element.17), channel_id=1, source_target_pairs={{1,0},{2,1},{3,2},{4,3},{5,4},{6,5},{7,6},{8,7},{9,8},{10,9},{11,1... | collective-permute-start | bytes 393224 | tf_op jit(solution)/shard_map/ppermute | solution.py:23
  173.7 12.5 %collective-permute-start.11 = (f32[4,64,128]{2,1,0:T(8,128)S(1)}, f32[4,64,128]{2,1,0:T(8,128)S(1)}, u32[]{:S(2)}, u32[]{:S(2)}) collective-permute-start(f32[4,64,128]{2,1,0:T(8,128)S(1)} %get-tuple-element.17), channel_id=1, source_target_pairs={{0,1},{1,2},{2,3},{3,4},{4,5},{5,6},{6,7},{7,8},{8,9},{9,10},{10,1... | collective-permute-start | bytes 393224 | tf_op jit(solution)/shard_map/ppermute | solution.py:20
  177.9 13.6 %collective-permute-start.27 = (f32[4,64,128]{2,1,0:T(8,128)S(1)}, f32[4,64,128]{2,1,0:T(8,128)S(1)}, u32[]{:S(2)}, u32[]{:S(2)}) collective-permute-start(f32[4,64,128]{2,1,0:T(8,128)S(1)} %bitcast.70), channel_id=1, source_target_pairs={{0,1},{1,2},{2,3},{3,4},{4,5},{5,6},{6,7},{7,8},{8,9},{9,10},{10,1... | collective-permute-start | bytes 393224 | tf_op jit(solution)/shard_map/ppermute | solution.py:20
  179.8 11.7 %collective-permute-start.26 = (f32[4,64,128]{2,1,0:T(8,128)S(1)}, f32[4,64,128]{2,1,0:T(8,128)S(1)}, u32[]{:S(2)}, u32[]{:S(2)}) collective-permute-start(f32[4,64,128]{2,1,0:T(8,128)S(1)} %bitcast.71), channel_id=1, source_target_pairs={{1,0},{2,1},{3,2},{4,3},{5,4},{6,5},{7,6},{8,7},{9,8},{10,9},{11,1... | collective-permute-start | bytes 393224 | tf_op jit(solution)/shard_map/ppermute | solution.py:23
  187.1 15.1 %collective-permute-start.12 = (f32[4,64,128]{2,1,0:T(8,128)S(1)}, f32[4,64,128]{2,1,0:T(8,128)S(1)}, u32[]{:S(2)}, u32[]{:S(2)}) collective-permute-start(f32[4,64,128]{2,1,0:T(8,128)S(1)} %get-tuple-element.15), channel_id=1, source_target_pairs={{1,0},{2,1},{3,2},{4,3},{5,4},{6,5},{7,6},{8,7},{9,8},{10,9},{11,1... | collective-permute-start | bytes 393224 | tf_op jit(solution)/shard_map/ppermute | solution.py:23
  189.5 12.7 %collective-permute-start.13 = (f32[4,64,128]{2,1,0:T(8,128)S(1)}, f32[4,64,128]{2,1,0:T(8,128)S(1)}, u32[]{:S(2)}, u32[]{:S(2)}) collective-permute-start(f32[4,64,128]{2,1,0:T(8,128)S(1)} %get-tuple-element.15), channel_id=1, source_target_pairs={{0,1},{1,2},{2,3},{3,4},{4,5},{5,6},{6,7},{7,8},{8,9},{9,10},{10,1... | collective-permute-start | bytes 393224 | tf_op jit(solution)/shard_map/ppermute | solution.py:20
  193.8 13.8 %collective-permute-start.29 = (f32[4,64,128]{2,1,0:T(8,128)S(1)}, f32[4,64,128]{2,1,0:T(8,128)S(1)}, u32[]{:S(2)}, u32[]{:S(2)}) collective-permute-start(f32[4,64,128]{2,1,0:T(8,128)S(1)} %bitcast.77), channel_id=1, source_target_pairs={{0,1},{1,2},{2,3},{3,4},{4,5},{5,6},{6,7},{7,8},{8,9},{9,10},{10,1... | collective-permute-start | bytes 393224 | tf_op jit(solution)/shard_map/ppermute | solution.py:20
  195.9 11.7 %collective-permute-start.28 = (f32[4,64,128]{2,1,0:T(8,128)S(1)}, f32[4,64,128]{2,1,0:T(8,128)S(1)}, u32[]{:S(2)}, u32[]{:S(2)}) collective-permute-start(f32[4,64,128]{2,1,0:T(8,128)S(1)} %bitcast.78), channel_id=1, source_target_pairs={{1,0},{2,1},{3,2},{4,3},{5,4},{6,5},{7,6},{8,7},{9,8},{10,9},{11,1... | collective-permute-start | bytes 393224 | tf_op jit(solution)/shard_map/ppermute | solution.py:23
  203.2 14.9 %collective-permute-start.14 = (f32[4,64,128]{2,1,0:T(8,128)S(1)}, f32[4,64,128]{2,1,0:T(8,128)S(1)}, u32[]{:S(2)}, u32[]{:S(2)}) collective-permute-start(f32[4,64,128]{2,1,0:T(8,128)S(1)} %get-tuple-element.13), channel_id=1, source_target_pairs={{1,0},{2,1},{3,2},{4,3},{5,4},{6,5},{7,6},{8,7},{9,8},{10,9},{11,1... | collective-permute-start | bytes 393224 | tf_op jit(solution)/shard_map/ppermute | solution.py:23
  205.6 12.5 %collective-permute-start.15 = (f32[4,64,128]{2,1,0:T(8,128)S(1)}, f32[4,64,128]{2,1,0:T(8,128)S(1)}, u32[]{:S(2)}, u32[]{:S(2)}) collective-permute-start(f32[4,64,128]{2,1,0:T(8,128)S(1)} %get-tuple-element.13), channel_id=1, source_target_pairs={{0,1},{1,2},{2,3},{3,4},{4,5},{5,6},{6,7},{7,8},{8,9},{9,10},{10,1... | collective-permute-start | bytes 393224 | tf_op jit(solution)/shard_map/ppermute | solution.py:20
  209.8 11.1 %collective-permute-start.31 = (f32[4,64,128]{2,1,0:T(8,128)S(1)}, f32[4,64,128]{2,1,0:T(8,128)S(1)}, u32[]{:S(2)}, u32[]{:S(2)}) collective-permute-start(f32[4,64,128]{2,1,0:T(8,128)S(1)} %bitcast.84), channel_id=1, source_target_pairs={{0,1},{1,2},{2,3},{3,4},{4,5},{5,6},{6,7},{7,8},{8,9},{9,10},{10,1... | collective-permute-start | bytes 393224 | tf_op jit(solution)/shard_map/ppermute | solution.py:20
  211.8 9.2 %collective-permute-start.30 = (f32[4,64,128]{2,1,0:T(8,128)S(1)}, f32[4,64,128]{2,1,0:T(8,128)S(1)}, u32[]{:S(2)}, u32[]{:S(2)}) collective-permute-start(f32[4,64,128]{2,1,0:T(8,128)S(1)} %bitcast.85), channel_id=1, source_target_pairs={{1,0},{2,1},{3,2},{4,3},{5,4},{6,5},{7,6},{8,7},{9,8},{10,9},{11,1... | collective-permute-start | bytes 393224 | tf_op jit(solution)/shard_map/ppermute | solution.py:23
  220.2 0.7 copy-start.3
  223.2 0.8 copy-start
Sparse Core Ops, SparseCore 0:
  221.0 120.6 all-reduce.17
where the time goes:
time: 351 us; the launch traced here: 350 us
  starting transfers between devices  126 us (36%)
  waiting for transfers between devices  124 us (35%)
  blocking collectives  46.4 us (13%)
  other arithmetic  28.7 us (8%)
  between operations  15.6 us (4%)
  local copies, waits for them, and re-layouts  9.78 us (3%)
    psum x1, waiting for transfers between devices, shards(): total = lax.psum(placed, 'shot')  118 us
    ppermute x16, starting transfers between devices, padded_2(): lax.ppermute(lax.slice_in_dim(block, 0, width, axis=dim), axis, backward)  71.3 us
    all_gather x1, blocking collectives, shards(): whole_rows = lax.all_gather(squared_courant, 'shot', axis=1, tiled=True)  46.4 us
    ppermute x16, starting transfers between devices, padded_2(): lax.ppermute(lax.slice_in_dim(block, block.shape[dim] - width, None, axis...  31.6 us
    all_to_all x1, starting transfers between devices, shards(): lax.all_to_all(receiver_cells, 'dom', split_axis=2, concat_axis=2, tiled=...  12.1 us
    scatter-add x8, other arithmetic, shards(): adj_next.reshape(-1).at[index].add(arrived[0, moment])  10.8 us
    all_to_all x1, starting transfers between devices, shards(): lax.all_to_all(masked, 'dom', split_axis=2, concat_axis=2, tiled=True)  10.7 us
  transfers between devices with their start and end apart: 35, of which 2 were waited for; matrix products, arithmetic and copies ran while one was open for 10% of the time, Pallas kernels for 0%

commit v1 on v0

v1 whole, which is shorter than its diff:
```python
import functools

import jax
import jax.numpy as jnp
from jax import lax
from jax.experimental import pallas as pl
from jax.experimental.pallas import tpu as pltpu
from jax.sharding import PartitionSpec as P

STEPS = 8
COEFFS = (-205.0 / 72.0, 8.0 / 5.0, -1.0 / 5.0, 8.0 / 315.0, -1.0 / 560.0)
MESH = pl.DeviceIdType.MESH
ROWS = pl.ds(8, 64)
OWN = pl.ds(4, 4)


def remote(src, dst, send, recv, where):
    return pltpu.make_async_remote_copy(
        src_ref=src, dst_ref=dst, send_sem=send, recv_sem=recv, device_id=where, device_id_type=MESH
    )


def lane_iota(shape):
    return lax.broadcasted_iota(jnp.int32, shape, len(shape) - 1)


def rolled(value, shift):
    return pltpu.roll(value, shift % 128, value.ndim - 1) if shift % 128 else value


def kernel(
    src_prev, src_now, adj_prev, adj_now, model, offsets, traces, cells, counts,
    src_out, adj_out, grad_out,
    x, lap, inj, courant, image, turned, pieces, grads, trace_send, trace_y, trace_row, slots, onehot,
    load_sem, halo_send, halo_recv, ty_send, ty_recv, tr_send, tr_recv, c_send, c_recv, g_send, g_recv,
):
    s = lax.axis_index("shot")
    d = lax.axis_index("dom")
    y, g = d // 8, d % 8
    sx, sz = s // 2, s % 2
    has_left, has_right = d > 0, d < 63
    off = offsets[0]

    loads = [
        pltpu.make_async_copy(ref.at[0], x.at[time, field, OWN, ROWS], load_sem.at[time, field])
        for time, field, ref in ((0, 0, src_now), (0, 1, adj_now), (1, 0, src_prev), (1, 1, adj_prev))
    ]

    for time in range(2):
        for field in range(2):
            for plane in range(12):
                if 4 <= plane < 8:
                    x[time, field, plane, 0:8] = jnp.zeros((8, 128), jnp.float32)
                    x[time, field, plane, 72:80] = jnp.zeros((8, 128), jnp.float32)
                else:
                    x[time, field, plane] = jnp.zeros((80, 128), jnp.float32)
    for copy in loads:
        copy.start()

    barrier = pltpu.get_barrier_semaphore()
    line = [(s, ((y + k) % 8) * 8 + g) for k in range(1, 8)]
    row = [(s, y * 8 + (g + k) % 8) for k in range(1, 8)]
    shot = {}
    for dz in range(2):
        for k in range(4):
            shot[dz, k] = (((sx + k) % 4) * 2 + (sz + dz) % 2, d)
    others = [key for key in shot if key != (0, 0)]
    for where in line + row + [shot[key] for key in others]:
        pl.semaphore_signal(barrier, inc=1, device_id=where, device_id_type=MESH)
    left_far = jnp.logical_and(has_left, g == 0)
    right_far = jnp.logical_and(has_right, g == 7)

    @pl.when(left_far)
    def _():
        pl.semaphore_signal(barrier, inc=1, device_id=(s, d - 1), device_id_type=MESH)

    @pl.when(right_far)
    def _():
        pl.semaphore_signal(barrier, inc=1, device_id=(s, d + 1), device_id_type=MESH)

    for plane in range(4):
        for half in range(2):
            pieces[0, 2 * plane + half] = model[plane, :, 128 * half : 128 * half + 128]
    pieces[0, 8] = jnp.full((8, 128), off, jnp.int32).astype(jnp.float32)
    spread = (lax.broadcasted_iota(jnp.int32, (64, 128), 0) == lane_iota((64, 128)) // 2).astype(jnp.float32)
    filled = jnp.broadcast_to(counts[0].astype(jnp.float32), (8, 64))
    live = (lane_iota((8, 128)) % 2).astype(jnp.float32) < jnp.dot(
        filled, spread, preferred_element_type=jnp.float32
    ) - 0.5
    trace_send[0:8] = jnp.where(live, traces[0], 0.0)
    trace_send[8:16] = jnp.broadcast_to(cells[0].astype(jnp.float32), (8, 128))

    far = left_far.astype(jnp.int32) + right_far.astype(jnp.int32)
    pl.semaphore_wait(barrier, 21 + far)

    def to_right(time):
        return remote(
            x.at[time, :, OWN, ROWS], x.at[time, :, pl.ds(0, 4), ROWS],
            halo_send.at[time, 0], halo_recv.at[time, 0], (s, d + 1),
        )

    def to_left(time):
        return remote(
            x.at[time, :, OWN, ROWS], x.at[time, :, pl.ds(8, 4), ROWS],
            halo_send.at[time, 1], halo_recv.at[time, 1], (s, d - 1),
        )

    def send_halos(time):
        @pl.when(has_right)
        def _():
            to_right(time).start()

        @pl.when(has_left)
        def _():
            to_left(time).start()

    def sent_halos(time):
        @pl.when(has_right)
        def _():
            to_right(time).wait_send()

        @pl.when(has_left)
        def _():
            to_left(time).wait_send()

    def got_halos(time):
        @pl.when(has_left)
        def _():
            to_right(time).wait_recv()

        @pl.when(has_right)
        def _():
            to_left(time).wait_recv()

    first = [
        remote(trace_send, trace_y.at[k], ty_send.at[k], ty_recv.at[k], line[k - 1]) for k in range(1, 8)
    ]
    for copy in first:
        copy.start()
    spread_1 = [
        remote(pieces.at[0], pieces.at[dz * 4 + k], c_send.at[dz * 4 + k], c_recv.at[dz * 4 + k], shot[dz, k])
        for dz, k in ((1, 0), (0, 1), (0, 2), (0, 3))
    ]
    for copy in spread_1:
        copy.start()
    loads[0].wait()
    loads[1].wait()
    send_halos(0)

    trace_y[0] = trace_send[...]
    for copy in first:
        copy.wait_recv()
    lane = lane_iota((16, 128))
    packed = jnp.zeros((16, 128), jnp.float32)
    for k in range(8):
        packed = packed + jnp.where(lane // 16 == (y + 8 - k) % 8, rolled(trace_y[k], -16 * k), 0.0)
    trace_row[0] = packed
    second = [
        remote(trace_row.at[0], trace_row.at[k], tr_send.at[k], tr_recv.at[k], row[k - 1]) for k in range(1, 8)
    ]
    for copy in second:
        copy.start()
    spread_1[0].wait_recv()
    spread_2 = [
        remote(pieces.at[4], pieces.at[4 + k], c_send.at[4 + k], c_recv.at[4 + k], shot[0, k]) for k in range(1, 4)
    ]
    for copy in spread_2:
        copy.start()
    for copy in second:
        copy.wait_recv()
    own = jnp.zeros((16, 128), jnp.float32)
    for k in range(8):
        own = own + jnp.where((lane // 2) % 8 == (g + 8 - k) % 8, rolled(trace_row[k], -2 * k), 0.0)
    slots[...] = own
    cell = own[8:9].astype(jnp.int32)
    onehot[...] = (
        lax.broadcasted_iota(jnp.int32, (256, 128), 0) == jnp.broadcast_to(cell >> 7, (256, 128))
    ).astype(jnp.float32).astype(jnp.bfloat16)
    for copy in spread_1[1:] + spread_2:
        copy.wait_recv()
    at = lane_iota((8, 128)) < 128 - off
    turn_back = lax.rem(128 - off, 128)
    for dz in range(2):
        for k in range(4):
            j = ((sx + 4 - k) % 4) * 2 + (sz + dz) % 2
            for plane in range(4):
                low = pltpu.roll(pieces[dz * 4 + k, 2 * plane], turn_back, 1)
                high = pltpu.roll(pieces[dz * 4 + k, 2 * plane + 1], turn_back, 1)
                courant[plane, pl.ds(pl.multiple_of(j * 8, 8), 8)] = jnp.where(at, low, high)
    loads[2].wait()
    loads[3].wait()
    for plane in range(4):
        image[plane] = jnp.zeros((64, 128), jnp.float32)

    lanes = lane_iota((64, 128))

    @pl.loop(0, STEPS)
    def _(t):
        now = t % 2
        new = 1 - now
        value = slots[pl.ds(t, 1)]
        cell_lane = slots[8:9].astype(jnp.int32) & 127
        hit = lax.broadcasted_iota(jnp.int32, (128, 128), 0) == jnp.broadcast_to(cell_lane, (128, 128))
        placed = jnp.where(hit, jnp.broadcast_to(value, (128, 128)), 0.0)
        high = placed.astype(jnp.bfloat16)
        low = (placed - high.astype(jnp.float32)).astype(jnp.bfloat16)
        dims = (((1,), (1,)), ((), ()))
        inj[...] = lax.dot_general(
            onehot[...], high, dims, preferred_element_type=jnp.float32
        ) + lax.dot_general(onehot[...], low, dims, preferred_element_type=jnp.float32)
        for field in range(2):
            for plane in range(4):
                center = x[now, field, 4 + plane, ROWS]
                total = 3.0 * COEFFS[0] * center
                for reach in range(1, 5):
                    pair = x[now, field, 4 + plane, pl.ds(8 + reach, 64)] + x[now, field, 4 + plane, pl.ds(8 - reach, 64)]
                    pair = pair + jnp.where(lanes >= reach, rolled(center, reach), 0.0)
                    pair = pair + jnp.where(lanes < 128 - reach, rolled(center, -reach), 0.0)
                    for other in (plane - reach, plane + reach):
                        if 0 <= other < 4:
                            pair = pair + x[now, field, 4 + other, ROWS]
                    total = total + COEFFS[reach] * pair
                lap[field, plane] = total

        @pl.when(t > 0)
        def _():
            sent_halos(new)

        got_halos(now)
        for field in range(2):
            for plane in range(4):
                total = lap[field, plane]
                for reach in range(1, 5):
                    for other in (plane - reach, plane + reach):
                        if not 0 <= other < 4:
                            total = total + COEFFS[reach] * x[now, field, 4 + other, ROWS]
                center = x[now, field, 4 + plane, ROWS]
                following = 2.0 * center - x[new, field, 4 + plane, ROWS] + courant[plane] * total
                if field == 0:
                    image[plane] += x[now, 1, 4 + plane, ROWS] * total
                else:
                    following = following + inj[64 * plane : 64 * plane + 64]
                x[new, field, 4 + plane, ROWS] = following

        @pl.when(t < STEPS - 1)
        def _():
            send_halos(new)

    sent_halos((STEPS - 1) % 2)

    turn = lax.rem(off, 128)
    for plane in range(4):
        turned[plane] = pltpu.roll(image[plane] * (1.0 / STEPS), turn, 1)
    grad_copies = []
    for dz, k in others:
        j = ((sx + k) % 4) * 2 + (sz + dz) % 2
        grad_copies.append(
            remote(
                turned.at[:, pl.ds(pl.multiple_of(j * 8, 8), 8)], grads.at[dz * 4 + k],
                g_send.at[dz * 4 + k], g_recv.at[dz * 4 + k], shot[dz, k],
            )
        )
    for copy in grad_copies:
        copy.start()
    src_out[0] = x[STEPS % 2, 0, OWN, ROWS]
    adj_out[0] = x[STEPS % 2, 1, OWN, ROWS]
    for copy in grad_copies:
        copy.wait_recv()
    lane8 = lane_iota((8, 128)).astype(jnp.float32)
    for plane in range(4):
        mine = turned[plane, pl.ds(pl.multiple_of(s * 8, 8), 8)]
        low = jnp.where(lane8 >= pieces[0, 8], mine, 0.0)
        high = mine - low
        for dz, k in others:
            part = grads[dz * 4 + k, plane]
            start = pieces[dz * 4 + k, 8]
            low = low + jnp.where(lane8 >= start, part, 0.0)
            high = high + jnp.where(lane8 < start, part, 0.0)
        grad_out[plane, :, 0:128] = low
        grad_out[plane, :, 128:256] = high
    for copy in first + second + spread_1 + spread_2 + grad_copies:
        copy.wait_send()


def shards(source_prev, source_now, adjoint_prev, adjoint_now, squared_courant, offsets, traces, receiver_cells, counts):
    field = jax.ShapeDtypeStruct(source_now.shape, jnp.float32)
    any_spec = pl.BlockSpec(memory_space=pl.ANY)
    vmem = pl.BlockSpec(memory_space=pltpu.VMEM)
    f32 = jnp.float32
    return pl.pallas_call(
        kernel,
        out_shape=(field, field, jax.ShapeDtypeStruct(squared_courant.shape, f32)),
        in_specs=[any_spec] * 4 + [vmem, pl.BlockSpec(memory_space=pltpu.SMEM), vmem, vmem, vmem],
        out_specs=(vmem, vmem, vmem),
        scratch_shapes=[
            pltpu.VMEM((2, 2, 12, 80, 128), f32),
            pltpu.VMEM((2, 4, 64, 128), f32),
            pltpu.VMEM((256, 128), f32),
            pltpu.VMEM((4, 64, 128), f32),
            pltpu.VMEM((4, 64, 128), f32),
            pltpu.VMEM((4, 64, 128), f32),
            pltpu.VMEM((8, 9, 8, 128), f32),
            pltpu.VMEM((8, 4, 8, 128), f32),
            pltpu.VMEM((16, 128), f32),
            pltpu.VMEM((8, 16, 128), f32),
            pltpu.VMEM((8, 16, 128), f32),
            pltpu.VMEM((16, 128), f32),
            pltpu.VMEM((256, 128), jnp.bfloat16),
            pltpu.SemaphoreType.DMA((2, 2)),
            pltpu.SemaphoreType.DMA((2, 2)),
            pltpu.SemaphoreType.DMA((2, 2)),
            pltpu.SemaphoreType.DMA((8,)),
            pltpu.SemaphoreType.DMA((8,)),
            pltpu.SemaphoreType.DMA((8,)),
            pltpu.SemaphoreType.DMA((8,)),
            pltpu.SemaphoreType.DMA((8,)),
            pltpu.SemaphoreType.DMA((8,)),
            pltpu.SemaphoreType.DMA((8,)),
            pltpu.SemaphoreType.DMA((8,)),
        ],
        compiler_params=pltpu.CompilerParams(
            collective_id=0, has_side_effects=True, vmem_limit_bytes=40 * 1024 * 1024
        ),
    )(source_prev, source_now, adjoint_prev, adjoint_now, squared_courant, offsets, traces, receiver_cells, counts)


def solution(mesh):
    placed = (
        P("shot", "dom", None, None),
        P("shot", "dom", None, None),
        P("shot", "dom", None, None),
        P("shot", "dom", None, None),
        P("dom", "shot", None),
        P("shot"),
        P("shot", None, "dom"),
        P("shot", None, "dom"),
        P("shot", "dom", None),
    )
    return jax.shard_map(
        shards,
        mesh=mesh,
        in_specs=placed,
        out_specs=(
            P("shot", "dom", None, None),
            P("shot", "dom", None, None),
            P("dom", "shot", None),
        ),
        check_vma=False,
    )
```

time: 351 us -> 94.5 us (0.27)
  the two profiles are of different devices: /device:TPU:16 before, /device:TPU:104 now
where the time goes in v1:
time: 94.5 us; the launch traced here: 94.2 us
  Pallas kernels  85.9 us (91%)
  local copies, waits for them, and re-layouts  6.99 us (7%)
  between operations  1.35 us (1%)
    pallas_call x1, Pallas kernels, shards(): pl.pallas_call(kernel, out_shape=(field, field, jax.ShapeDtypeStruct(squa...  85.9 us
    unnamed x19, local copies, waits for them, and re-layouts  6.99 us

profile of v1, /device:TPU:104, one launch (start us, length us, event | category | flops | bytes accessed | tf_op | source)
XLA Modules:
  0.0 94.2 jit_solution(13467508090776334103)
XLA Ops:
  0.6 0.0 copy-start.7
  0.6 0.0 copy-start.6
  1.3 0.0 copy-done.7
  1.3 0.0 copy-done.6
  1.3 0.0 copy-start
  1.3 0.9 copy-done
  2.2 0.0 copy-start.1
  2.2 0.9 copy-done.1
  3.1 0.0 copy-start.2
  3.1 0.9 copy-done.2
  4.1 0.0 copy-start.3
  4.1 0.9 copy-done.3
  5.0 0.0 copy-start.4
  5.0 0.8 copy-done.4
  5.7 0.0 copy-start.5
  5.7 0.7 copy-done.5
  6.4 85.9 %shard_map.112 = (f32[1,4,64,128]{3,2,1,0:T(8,128)S(1)}, f32[1,4,64,128]{3,2,1,0:T(8,128)S(1)}, f32[4,8,256]{2,1,0:T(8,128)S(1)}) custom-call(f32[1,4,64,128]{3,2,1,0:T(8,128)S(1)} %copy-done, f32[1,4,64,128]{3,2,1,0:T(8,128)S(1)} %copy-done.1, f32[1,4,64,128]{3,2,1,0:T(8,128)S(1)} %copy-done.2, f32[1,4,64,128]{3,2,1,0:T(8,128)S(1)} %copy-done.3, ...), custom_call_target="tpu_custom_call" | custom-call | tf_op jit(solution)/shard_map/pallas_call | solution.py:290
  92.3 0.7 copy.16
  92.9 0.7 copy.17
  93.6 0.6 copy.18
Async XLA Ops:
  0.6 0.7 copy-start.7
  0.6 0.7 copy-start.6
  1.3 0.9 copy-start
  2.2 0.9 copy-start.1
  3.1 0.9 copy-start.2
  4.1 0.9 copy-start.3
  5.0 0.8 copy-start.4
  5.7 0.7 copy-start.5

commit v2 on v1

v2 whole, which is shorter than its diff:
```python
import functools

import jax
import jax.numpy as jnp
from jax import lax
from jax.experimental import pallas as pl
from jax.experimental.pallas import tpu as pltpu
from jax.sharding import PartitionSpec as P

STEPS = 8
COEFFS = (-205.0 / 72.0, 8.0 / 5.0, -1.0 / 5.0, 8.0 / 315.0, -1.0 / 560.0)
MESH = pl.DeviceIdType.MESH
ROWS = pl.ds(8, 64)
OWN = pl.ds(4, 4)


def remote(src, dst, send, recv, where):
    return pltpu.make_async_remote_copy(
        src_ref=src, dst_ref=dst, send_sem=send, recv_sem=recv, device_id=where, device_id_type=MESH
    )


def lane_iota(shape):
    return lax.broadcasted_iota(jnp.int32, shape, len(shape) - 1)


def rolled(value, shift):
    return pltpu.roll(value, shift % 128, value.ndim - 1) if shift % 128 else value


def kernel(
    src_prev, src_now, adj_prev, adj_now, model_in, offsets_in, traces_in, cells_in, counts_in,
    src_out, adj_out, grad_out,
    x, lap, inj, courant, image, turned, pieces, grads, trace_send, trace_y, trace_row, slots, onehot,
    traces, cells, counts, offsets, summed,
    load_sem, small_sem, halo_send, halo_recv, ty_send, ty_recv, tr_send, tr_recv, c_send, c_recv, g_send, g_recv,
):
    s = lax.axis_index("shot")
    d = lax.axis_index("dom")
    y, g = d // 8, d % 8
    sx, sz = s // 2, s % 2
    has_left, has_right = d > 0, d < 63

    loads = [
        pltpu.make_async_copy(ref.at[0], x.at[time, field, OWN, ROWS], load_sem.at[time, field])
        for time, field, ref in ((0, 0, src_now), (0, 1, adj_now), (1, 0, src_prev), (1, 1, adj_prev))
    ]

    halves = [
        pltpu.make_async_copy(
            model_in.at[:, :, pl.ds(128 * half, 128)], pieces.at[0, pl.ds(4 * half, 4)], small_sem.at[half]
        )
        for half in range(2)
    ]
    small = [
        pltpu.make_async_copy(ref.at[0], scratch, small_sem.at[2 + i])
        for i, (ref, scratch) in enumerate(((traces_in, traces), (cells_in, cells), (counts_in, counts)))
    ] + [pltpu.make_async_copy(offsets_in, offsets, small_sem.at[5])]
    barrier = pltpu.get_barrier_semaphore()
    line = [(s, ((y + k) % 8) * 8 + g) for k in range(1, 8)]
    row = [(s, y * 8 + (g + k) % 8) for k in range(1, 8)]
    shot = {}
    for dz in range(2):
        for k in range(4):
            shot[dz, k] = (((sx + k) % 4) * 2 + (sz + dz) % 2, d)
    others = [key for key in shot if key != (0, 0)]
    for where in line + row + [shot[key] for key in others]:
        pl.semaphore_signal(barrier, inc=1, device_id=where, device_id_type=MESH)
    left_far = jnp.logical_and(has_left, g == 0)
    right_far = jnp.logical_and(has_right, g == 7)

    @pl.when(left_far)
    def _():
        pl.semaphore_signal(barrier, inc=1, device_id=(s, d - 1), device_id_type=MESH)

    @pl.when(right_far)
    def _():
        pl.semaphore_signal(barrier, inc=1, device_id=(s, d + 1), device_id_type=MESH)

    for copy in small + halves + loads:
        copy.start()

    for time in range(2):
        for field in range(2):
            for plane in range(4, 8):
                x[time, field, plane, 0:8] = jnp.zeros((8, 128), jnp.float32)
                x[time, field, plane, 72:80] = jnp.zeros((8, 128), jnp.float32)

    def clear(first_plane):
        for time in range(2):
            for field in range(2):
                for plane in range(first_plane, first_plane + 4):
                    x[time, field, plane, ROWS] = jnp.zeros((64, 128), jnp.float32)

    @pl.when(jnp.logical_not(has_left))
    def _():
        clear(0)

    @pl.when(jnp.logical_not(has_right))
    def _():
        clear(8)

    for copy in small:
        copy.wait()
    off = offsets[0]
    pieces[0, 8] = jnp.full((8, 128), off, jnp.int32).astype(jnp.float32)
    spread = (lax.broadcasted_iota(jnp.int32, (64, 128), 0) == lane_iota((64, 128)) // 2).astype(jnp.float32)
    filled = jnp.broadcast_to(counts[...].astype(jnp.float32), (8, 64))
    live = (lane_iota((8, 128)) % 2).astype(jnp.float32) < jnp.dot(
        filled, spread, preferred_element_type=jnp.float32
    ) - 0.5
    trace_send[0:8] = jnp.where(live, traces[...], 0.0)
    trace_send[8:16] = jnp.broadcast_to(cells[...].astype(jnp.float32), (8, 128))

    far = left_far.astype(jnp.int32) + right_far.astype(jnp.int32)
    pl.semaphore_wait(barrier, 21 + far)

    def to_right(time, field):
        return remote(
            x.at[time, field, OWN, ROWS], x.at[time, field, pl.ds(0, 4), ROWS],
            halo_send.at[time, 0, field], halo_recv.at[time, 0, field], (s, d + 1),
        )

    def to_left(time, field):
        return remote(
            x.at[time, field, OWN, ROWS], x.at[time, field, pl.ds(8, 4), ROWS],
            halo_send.at[time, 1, field], halo_recv.at[time, 1, field], (s, d - 1),
        )

    def send_halos(time, field):
        @pl.when(has_right)
        def _():
            to_right(time, field).start()

        @pl.when(has_left)
        def _():
            to_left(time, field).start()

    def sent_halos(time, field):
        @pl.when(has_right)
        def _():
            to_right(time, field).wait_send()

        @pl.when(has_left)
        def _():
            to_left(time, field).wait_send()

    def got_halos(time, field):
        @pl.when(has_left)
        def _():
            to_right(time, field).wait_recv()

        @pl.when(has_right)
        def _():
            to_left(time, field).wait_recv()

    lanes = lane_iota((64, 128))

    def inside(time, field):
        for plane in range(4):
            center = x[time, field, 4 + plane, ROWS]
            total = 3.0 * COEFFS[0] * center
            for reach in range(1, 5):
                pair = x[time, field, 4 + plane, pl.ds(8 + reach, 64)] + x[time, field, 4 + plane, pl.ds(8 - reach, 64)]
                pair = pair + jnp.where(lanes >= reach, rolled(center, reach), 0.0)
                pair = pair + jnp.where(lanes < 128 - reach, rolled(center, -reach), 0.0)
                for other in (plane - reach, plane + reach):
                    if 0 <= other < 4:
                        pair = pair + x[time, field, 4 + other, ROWS]
                total = total + COEFFS[reach] * pair
            lap[field, plane] = total

    def injection(t):
        value = slots[pl.ds(t, 1)]
        cell_lane = slots[8:9].astype(jnp.int32) & 127
        hit = lax.broadcasted_iota(jnp.int32, (128, 128), 0) == jnp.broadcast_to(cell_lane, (128, 128))
        placed = jnp.where(hit, jnp.broadcast_to(value, (128, 128)), 0.0)
        high = placed.astype(jnp.bfloat16)
        low = (placed - high.astype(jnp.float32)).astype(jnp.bfloat16)
        dims = (((1,), (1,)), ((), ()))
        inj[...] = lax.dot_general(
            onehot[...], high, dims, preferred_element_type=jnp.float32
        ) + lax.dot_general(onehot[...], low, dims, preferred_element_type=jnp.float32)

    def advance(now, new, field):
        for plane in range(4):
            total = lap[field, plane]
            for reach in range(1, 5):
                for other in (plane - reach, plane + reach):
                    if not 0 <= other < 4:
                        total = total + COEFFS[reach] * x[now, field, 4 + other, ROWS]
            center = x[now, field, 4 + plane, ROWS]
            following = 2.0 * center - x[new, field, 4 + plane, ROWS] + courant[plane] * total
            if field == 0:
                image[plane] += x[now, 1, 4 + plane, ROWS] * total
            else:
                following = following + inj[64 * plane : 64 * plane + 64]
            x[new, field, 4 + plane, ROWS] = following

    spread_1 = [
        remote(pieces.at[0], pieces.at[dz * 4 + k], c_send.at[dz * 4 + k], c_recv.at[dz * 4 + k], shot[dz, k])
        for dz, k in ((1, 0), (0, 1), (0, 2), (0, 3))
    ]
    for copy in halves:
        copy.wait()
    for copy in spread_1:
        copy.start()
    loads[0].wait()
    send_halos(0, 0)
    first = [
        remote(trace_send, trace_y.at[k], ty_send.at[k], ty_recv.at[k], line[k - 1]) for k in range(1, 8)
    ]
    for copy in first:
        copy.start()
    loads[1].wait()
    send_halos(0, 1)
    inside(0, 0)

    trace_y[0] = trace_send[...]
    spread_1[0].wait_recv()
    spread_2 = [
        remote(pieces.at[4], pieces.at[4 + k], c_send.at[4 + k], c_recv.at[4 + k], shot[0, k]) for k in range(1, 4)
    ]
    for copy in spread_2:
        copy.start()
    for copy in first:
        copy.wait_recv()
    lane = lane_iota((16, 128))
    packed = jnp.zeros((16, 128), jnp.float32)
    for k in range(8):
        packed = packed + jnp.where(lane // 16 == (y + 8 - k) % 8, rolled(trace_y[k], -16 * k), 0.0)
    trace_row[0] = packed
    along = [
        remote(trace_row.at[0], trace_row.at[k], tr_send.at[k], tr_recv.at[k], row[k - 1]) for k in range(1, 8)
    ]
    for copy in along:
        copy.start()
    inside(0, 1)
    for copy in spread_1[1:] + spread_2:
        copy.wait_recv()
    at = lane_iota((8, 128)) < 128 - off
    turn_back = lax.rem(128 - off, 128)
    for dz in range(2):
        for k in range(4):
            j = ((sx + 4 - k) % 4) * 2 + (sz + dz) % 2
            for plane in range(4):
                low = pltpu.roll(pieces[dz * 4 + k, plane], turn_back, 1)
                high = pltpu.roll(pieces[dz * 4 + k, 4 + plane], turn_back, 1)
                courant[plane, pl.ds(pl.multiple_of(j * 8, 8), 8)] = jnp.where(at, low, high)
    loads[2].wait()
    loads[3].wait()
    for plane in range(4):
        image[plane] = jnp.zeros((64, 128), jnp.float32)

    got_halos(0, 0)
    advance(0, 1, 0)
    send_halos(1, 0)
    inside(1, 0)
    for copy in along:
        copy.wait_recv()
    own = jnp.zeros((16, 128), jnp.float32)
    for k in range(8):
        own = own + jnp.where((lane // 2) % 8 == (g + 8 - k) % 8, rolled(trace_row[k], -2 * k), 0.0)
    slots[...] = own
    cell = own[8:9].astype(jnp.int32)
    onehot[...] = (
        lax.broadcasted_iota(jnp.int32, (256, 128), 0) == jnp.broadcast_to(cell >> 7, (256, 128))
    ).astype(jnp.float32).astype(jnp.bfloat16)
    injection(0)
    got_halos(0, 1)
    advance(0, 1, 1)
    send_halos(1, 1)
    inside(1, 1)
    injection(1)

    @pl.loop(1, STEPS - 1)
    def _(t):
        now = t % 2
        new = 1 - now
        for field in range(2):
            sent_halos(new, field)
            got_halos(now, field)
            advance(now, new, field)
            send_halos(new, field)
            inside(new, field)
        injection(t + 1)

    now = (STEPS - 1) % 2
    new = 1 - now
    results = [
        pltpu.make_async_copy(x.at[new, field, OWN, ROWS], ref.at[0], small_sem.at[field])
        for field, ref in enumerate((src_out, adj_out))
    ]
    sent_halos(new, 0)
    got_halos(now, 0)
    advance(now, new, 0)

    turn = lax.rem(off, 128)
    for plane in range(4):
        turned[plane] = pltpu.roll(image[plane] * (1.0 / STEPS), turn, 1)
    grad_copies = []
    for dz, k in others:
        j = ((sx + k) % 4) * 2 + (sz + dz) % 2
        grad_copies.append(
            remote(
                turned.at[:, pl.ds(pl.multiple_of(j * 8, 8), 8)], grads.at[dz * 4 + k],
                g_send.at[dz * 4 + k], g_recv.at[dz * 4 + k], shot[dz, k],
            )
        )
    for copy in grad_copies:
        copy.start()
    results[0].start()
    sent_halos(new, 1)
    got_halos(now, 1)
    advance(now, new, 1)
    results[1].start()
    for copy in grad_copies:
        copy.wait_recv()
    lane8 = lane_iota((8, 128)).astype(jnp.float32)
    for plane in range(4):
        mine = turned[plane, pl.ds(pl.multiple_of(s * 8, 8), 8)]
        low = jnp.where(lane8 >= pieces[0, 8], mine, 0.0)
        high = mine - low
        for dz, k in others:
            part = grads[dz * 4 + k, plane]
            start = pieces[dz * 4 + k, 8]
            low = low + jnp.where(lane8 >= start, part, 0.0)
            high = high + jnp.where(lane8 < start, part, 0.0)
        summed[plane, :, 0:128] = low
        summed[plane, :, 128:256] = high
    gradient = pltpu.make_async_copy(summed, grad_out, small_sem.at[2])
    gradient.start()
    for copy in first + along + spread_1 + spread_2 + grad_copies:
        copy.wait_send()
    for field in range(2):
        sent_halos(now, field)
    for copy in results + [gradient]:
        copy.wait()


def deliver(*refs):
    given, wanted, held, sems = refs[0:3], refs[3:6], refs[6:9], refs[9]
    into = [pltpu.make_async_copy(a, b, sems.at[0, i]) for i, (a, b) in enumerate(zip(given, held, strict=True))]
    out = [pltpu.make_async_copy(a, b, sems.at[1, i]) for i, (a, b) in enumerate(zip(held, wanted, strict=True))]
    for copy in into:
        copy.start()
    for i in range(3):
        into[i].wait()
        out[i].start()
    for copy in out:
        copy.wait()


def shards(source_prev, source_now, adjoint_prev, adjoint_now, squared_courant, offsets, traces, receiver_cells, counts):
    field = jax.ShapeDtypeStruct(source_now.shape, jnp.float32)
    hbm = pl.BlockSpec(memory_space=pltpu.HBM)
    f32 = jnp.float32
    results = pl.pallas_call(
        kernel,
        out_shape=(field, field, jax.ShapeDtypeStruct(squared_courant.shape, f32)),
        in_specs=[hbm] * 9,
        out_specs=(hbm, hbm, hbm),
        scratch_shapes=[
            pltpu.VMEM((2, 2, 12, 80, 128), f32),
            pltpu.VMEM((2, 4, 64, 128), f32),
            pltpu.VMEM((256, 128), f32),
            pltpu.VMEM((4, 64, 128), f32),
            pltpu.VMEM((4, 64, 128), f32),
            pltpu.VMEM((4, 64, 128), f32),
            pltpu.VMEM((8, 9, 8, 128), f32),
            pltpu.VMEM((8, 4, 8, 128), f32),
            pltpu.VMEM((16, 128), f32),
            pltpu.VMEM((8, 16, 128), f32),
            pltpu.VMEM((8, 16, 128), f32),
            pltpu.VMEM((16, 128), f32),
            pltpu.VMEM((256, 128), jnp.bfloat16),
            pltpu.VMEM((8, 128), f32),
            pltpu.VMEM((1, 128), jnp.int32),
            pltpu.VMEM((1, 64), jnp.int32),
            pltpu.SMEM((1,), jnp.int32),
            pltpu.VMEM((4, 8, 256), f32),
            pltpu.SemaphoreType.DMA((2, 2)),
            pltpu.SemaphoreType.DMA((6,)),
            pltpu.SemaphoreType.DMA((2, 2, 2)),
            pltpu.SemaphoreType.DMA((2, 2, 2)),
            pltpu.SemaphoreType.DMA((8,)),
            pltpu.SemaphoreType.DMA((8,)),
            pltpu.SemaphoreType.DMA((8,)),
            pltpu.SemaphoreType.DMA((8,)),
            pltpu.SemaphoreType.DMA((8,)),
            pltpu.SemaphoreType.DMA((8,)),
            pltpu.SemaphoreType.DMA((8,)),
            pltpu.SemaphoreType.DMA((8,)),
        ],
        compiler_params=pltpu.CompilerParams(
            collective_id=0, has_side_effects=True, vmem_limit_bytes=60 * 1024 * 1024
        ),
    )(source_prev, source_now, adjoint_prev, adjoint_now, squared_courant, offsets, traces, receiver_cells, counts)
    return pl.pallas_call(
        deliver,
        out_shape=tuple(jax.ShapeDtypeStruct(r.shape, f32) for r in results),
        in_specs=[hbm] * 3,
        out_specs=(hbm,) * 3,
        scratch_shapes=[pltpu.VMEM(r.shape, f32) for r in results] + [pltpu.SemaphoreType.DMA((2, 3))],
        compiler_params=pltpu.CompilerParams(vmem_limit_bytes=60 * 1024 * 1024),
    )(*results)


def solution(mesh):
    placed = (
        P("shot", "dom", None, None),
        P("shot", "dom", None, None),
        P("shot", "dom", None, None),
        P("shot", "dom", None, None),
        P("dom", "shot", None),
        P("shot"),
        P("shot", None, "dom"),
        P("shot", None, "dom"),
        P("shot", "dom", None),
    )
    return jax.shard_map(
        shards,
        mesh=mesh,
        in_specs=placed,
        out_specs=(
            P("shot", "dom", None, None),
            P("shot", "dom", None, None),
            P("dom", "shot", None),
        ),
        check_vma=False,
    )
```

time: 94.5 us -> 79.9 us (0.85)
  the two profiles are of different devices: /device:TPU:104 before, /device:TPU:33 now
where the time goes in v2:
time: 79.9 us; the launch traced here: 79.7 us
  Pallas kernels  78.4 us (98%)
  between operations  1.29 us (2%)
    pallas_call x1, Pallas kernels, shards(): pl.pallas_call(kernel, out_shape=(field, field, jax.ShapeDtypeStruct(squa...  76.7 us
    pallas_call x1, Pallas kernels, shards(): pl.pallas_call(deliver, out_shape=tuple((jax.ShapeDtypeStruct(r.shape, f3...  1.68 us

profile of v2, /device:TPU:33, one launch (start us, length us, event | category | flops | bytes accessed | tf_op | source)
XLA Modules:
  0.0 79.7 jit_solution(17021953469355344399)
XLA Ops:
  1.3 76.7 %shard_map.112 = (f32[1,4,64,128]{3,2,1,0:T(8,128)}, f32[1,4,64,128]{3,2,1,0:T(8,128)}, f32[4,8,256]{2,1,0:T(8,128)}) custom-call(f32[1,4,64,128]{3,2,1,0:T(8,128)} %src_prev.1, f32[1,4,64,128]{3,2,1,0:T(8,128)} %src_now.1, f32[1,4,64,128]{3,2,1,0:T(8,128)} %adj_prev.1, f32[1,4,64,128]{3,2,1,0:T(8,128)} %adj_now.1, f32[4,8,256]{2,1,0:T(8,128)} %model_in.1, ...), custom_call_target="tpu_custom_call" | custom-call | tf_op jit(solution)/shard_map/pallas_call | solution.py:358
  78.0 1.7 %shard_map.113 = (f32[1,4,64,128]{3,2,1,0:T(8,128)}, f32[1,4,64,128]{3,2,1,0:T(8,128)}, f32[4,8,256]{2,1,0:T(8,128)}) custom-call(f32[1,4,64,128]{3,2,1,0:T(8,128)} %get-tuple-element.6.refs_0_, f32[1,4,64,128]{3,2,1,0:T(8,128)} %get-tuple-element.7.refs_1_, f32[4,8,256]{2,1,0:T(8,128)} %get-tuple-element.8.refs_2_), custom_call_target="tpu_custom_call" | custom-call | tf_op jit(solution)/shard_map/pallas_call | solution.py:399

commit v3 on v2

v3 whole, which is shorter than its diff:
```python
import jax
import jax.numpy as jnp
from jax import lax
from jax.experimental import pallas as pl
from jax.experimental.pallas import tpu as pltpu
from jax.sharding import PartitionSpec as P

STEPS = 8
COEFFS = (-205.0 / 72.0, 8.0 / 5.0, -1.0 / 5.0, 8.0 / 315.0, -1.0 / 560.0)
MESH = pl.DeviceIdType.MESH
OWN_ROWS = pl.ds(16, 16)
ALL_ROWS = pl.ds(8, 32)
WAYS = ((1, 0), (-1, 0), (0, 1), (0, -1), (1, 1), (1, -1), (-1, 1), (-1, -1))


def remote(src, dst, send, recv, where):
    return pltpu.make_async_remote_copy(
        src_ref=src, dst_ref=dst, send_sem=send, recv_sem=recv, device_id=where, device_id_type=MESH
    )


def lane_iota(shape):
    return lax.broadcasted_iota(jnp.int32, shape, len(shape) - 1)


def rolled(value, shift):
    return pltpu.roll(value, shift % 128, value.ndim - 1) if shift % 128 else value


def laplace(ref, plane, first, rows):
    center = ref[plane, pl.ds(first, rows)]
    lanes = lane_iota((rows, 128))
    total = 3.0 * COEFFS[0] * center
    for reach in range(1, 5):
        pair = ref[plane + reach, pl.ds(first, rows)] + ref[plane - reach, pl.ds(first, rows)]
        pair = pair + ref[plane, pl.ds(first + reach, rows)] + ref[plane, pl.ds(first - reach, rows)]
        pair = pair + jnp.where(lanes >= reach, rolled(center, reach), 0.0)
        pair = pair + jnp.where(lanes < 128 - reach, rolled(center, -reach), 0.0)
        total = total + COEFFS[reach] * pair
    return center, total


def kernel(
    src_prev, src_now, adj_prev, adj_now, model_in, offsets_in, traces_in, cells_in, counts_in,
    src_out, adj_out, grad_out,
    n, m, cc, courant, image, lap, inj, pieces, grads, trace_send, trace_y, trace_row, slots, tables, onehot,
    traces, cells, counts, offsets, summed, outv,
    small_sem, relay_send, relay_recv, table_send, table_recv, halo_send, halo_recv, side_send, side_recv,
    ty_send, ty_recv, tr_send, tr_recv, c_send, c_recv, g_send, g_recv, o_send, o_recv,
):
    s = lax.axis_index("shot")
    d = lax.axis_index("dom")
    y, g = d // 8, d % 8
    z, c = g // 2, g % 2
    sx, sz = s // 2, s % 2
    xb = 2 * y + c
    hc = z // 2
    home = 2 * y + hc
    place = d % 4
    stays = hc == c

    def block(x_index, z_index):
        return (x_index // 2) * 8 + z_index * 2 + x_index % 2

    def here(shift):
        return y * 8 + ((z + shift) % 4) * 2 + hc

    halves = [
        pltpu.make_async_copy(
            model_in.at[:, :, pl.ds(128 * half, 128)], pieces.at[0, pl.ds(4 * half, 4)], small_sem.at[half]
        )
        for half in range(2)
    ]
    small = [
        pltpu.make_async_copy(ref.at[0], scratch, small_sem.at[2 + i])
        for i, (ref, scratch) in enumerate(((traces_in, traces), (cells_in, cells), (counts_in, counts)))
    ] + [pltpu.make_async_copy(offsets_in, offsets, small_sem.at[5])]
    for copy in small + halves:
        copy.start()

    tables[...] = jnp.zeros((6, 16, 128), jnp.float32)

    def clear_planes(first):
        for f in range(2):
            for plane in range(first, first + 8):
                for par in range(2):
                    n[par, f, plane] = jnp.zeros((48, 128), jnp.float32)
                m[f, plane] = jnp.zeros((48, 128), jnp.float32)
        for plane in range(4):
            cc[(0 if first == 0 else 20) + plane] = jnp.zeros((32, 128), jnp.float32)

    def clear_rows(first):
        for f in range(2):
            for plane in range(32):
                for par in range(2):
                    n[par, f, plane, first : first + 8] = jnp.zeros((8, 128), jnp.float32)
                m[f, plane, first : first + 8] = jnp.zeros((8, 128), jnp.float32)
        for plane in range(24):
            cc[plane, first - 8 : first] = jnp.zeros((8, 128), jnp.float32)

    for ended, clear, first in (
        (xb == 0, clear_planes, 0), (xb == 15, clear_planes, 24), (z == 0, clear_rows, 8), (z == 3, clear_rows, 32)
    ):
        @pl.when(ended)
        def _():
            clear(first)

    barrier = pltpu.get_barrier_semaphore()

    def greet(where):
        pl.semaphore_signal(barrier, inc=1, device_id=where, device_id_type=MESH)

    line = [(s, ((y + k) % 8) * 8 + g) for k in range(1, 8)]
    row = [(s, y * 8 + (g + k) % 8) for k in range(1, 8)]
    shot = {}
    for dz in range(2):
        for k in range(4):
            shot[dz, k] = (((sx + k) % 4) * 2 + (sz + dz) % 2, d)
    others = [key for key in shot if key != (0, 0)]
    for where in line + row + [shot[key] for key in others]:
        greet(where)
    beyond = jnp.where(c == 1, y < 7, y > 0)

    @pl.when(beyond)
    def _():
        for k in range(4):
            greet((s, jnp.where(c == 1, (y + 1) * 8, (y - 1) * 8 + 1) + 2 * k))

    own_gradient = jnp.logical_and(sx == z, stays)
    for k in range(8):
        if k:
            greet(((s + k) % 8, y * 8 + 2 * sx + hc))
        else:
            @pl.when(jnp.logical_not(own_gradient))
            def _():
                greet((s, y * 8 + 2 * sx + hc))

    expected = 21 + 4 * beyond.astype(jnp.int32) + 8 - own_gradient.astype(jnp.int32)
    for copy in small:
        copy.wait()
    off = offsets[0]
    pieces[0, 8] = jnp.full((8, 128), off, jnp.int32).astype(jnp.float32)
    for copy in halves:
        copy.wait()
    pl.semaphore_wait(barrier, expected)

    spread_1 = [
        remote(pieces.at[0], pieces.at[dz * 4 + k], c_send.at[dz * 4 + k], c_recv.at[dz * 4 + k], shot[dz, k])
        for dz, k in ((1, 0), (0, 1), (0, 2), (0, 3))
    ]
    for copy in spread_1:
        copy.start()

    def relay(array, source, target, base, rows, action):
        for k in range(4):
            src = source.at[:, pl.ds(pl.multiple_of(16 * ((z + k) % 4), 16), 16)]
            dst = target.at[pl.ds(base + 4 * place, 4), rows]
            copy = remote(src, dst, relay_send.at[array, k], relay_recv.at[array, place], (s, here(k)))
            if action == "start":
                if k:
                    copy.start()
                else:
                    @pl.when(stays)
                    def _():
                        pltpu.make_async_copy(src, dst, relay_recv.at[array, place]).start()

                    @pl.when(jnp.logical_not(stays))
                    def _():
                        copy.start()
            elif action == "sent":
                if k:
                    copy.wait_send()
                else:
                    @pl.when(jnp.logical_not(stays))
                    def _():
                        copy.wait_send()
            else:
                got = target.at[pl.ds(base + 4 * k, 4), rows]
                remote(got, got, relay_send.at[array, k], relay_recv.at[array, k], (s, here(k))).wait_recv()

    relays = (
        (0, src_now.at[0], n.at[0, 0], 8, OWN_ROWS),
        (1, adj_now.at[0], n.at[0, 1], 8, OWN_ROWS),
        (2, src_prev.at[0], m.at[0], 8, OWN_ROWS),
        (3, adj_prev.at[0], m.at[1], 8, OWN_ROWS),
        (4, courant, cc, 4, pl.ds(8, 16)),
    )
    relay(*relays[0], "start")
    relay(*relays[1], "start")

    def there(way):
        return jnp.logical_and(
            jnp.logical_and(xb + way[0] >= 0, xb + way[0] < 16), jnp.logical_and(z + way[1] >= 0, z + way[1] < 4)
        )

    def parts(way, depth):
        src_plane = {1: 24 - depth, -1: 8, 0: 8}[way[0]]
        dst_plane = {1: 8 - depth, -1: 24, 0: 8}[way[0]]
        planes = depth if way[0] else 16
        src_row = {1: 24, -1: 16, 0: 16}[way[1]]
        dst_row = {1: 8, -1: 32, 0: 16}[way[1]]
        rows = 8 if way[1] else 16
        return src_plane, dst_plane, planes, src_row, dst_row, rows

    def margin(i, target, depth, send, recv, plane_shift=0, row_shift=0):
        sp, dp, planes, sr, dr, rows = parts(WAYS[i], depth)
        return remote(
            target.at[pl.ds(sp - plane_shift, planes), pl.ds(sr - row_shift, rows)],
            target.at[pl.ds(dp - plane_shift, planes), pl.ds(dr - row_shift, rows)],
            send.at[i], recv.at[i], (s, block(xb + WAYS[i][0], z + WAYS[i][1])),
        )

    def halo(i, par, f):
        return margin(i, n.at[par, f], 4 if i >= 4 else 8, halo_send.at[par, f], halo_recv.at[par, f])

    def side(i, which):
        if which == 2:
            return margin(i, cc, 4, side_send.at[2], side_recv.at[2], 4, 8)
        return margin(i, m.at[which], 4, side_send.at[which], side_recv.at[which])

    def each_way(make, count, action):
        for i in range(count):
            if action == "got":
                sender = (-WAYS[i][0], -WAYS[i][1])

                @pl.when(there(sender))
                def _():
                    make(i).wait_recv()
            else:
                @pl.when(there(WAYS[i]))
                def _():
                    if action == "start":
                        make(i).start()
                    else:
                        make(i).wait_send()

    spread = (lax.broadcasted_iota(jnp.int32, (64, 128), 0) == lane_iota((64, 128)) // 2).astype(jnp.float32)
    filled = jnp.broadcast_to(counts[...].astype(jnp.float32), (8, 64))
    live = (lane_iota((8, 128)) % 2).astype(jnp.float32) < jnp.dot(
        filled, spread, preferred_element_type=jnp.float32
    ) - 0.5
    trace_send[0:8] = jnp.where(live, traces[...], 0.0)
    trace_send[8:16] = jnp.broadcast_to(cells[...].astype(jnp.float32), (8, 128))
    first = [
        remote(trace_send, trace_y.at[k], ty_send.at[k], ty_recv.at[k], line[k - 1]) for k in range(1, 8)
    ]
    for copy in first:
        copy.start()
    relay(*relays[2], "start")
    trace_y[0] = trace_send[...]

    spread_1[0].wait_recv()
    spread_2 = [
        remote(pieces.at[4], pieces.at[4 + k], c_send.at[4 + k], c_recv.at[4 + k], shot[0, k]) for k in range(1, 4)
    ]
    for copy in spread_2:
        copy.start()
    for copy in first:
        copy.wait_recv()
    lane = lane_iota((16, 128))
    packed = jnp.zeros((16, 128), jnp.float32)
    for k in range(8):
        packed = packed + jnp.where(lane // 16 == (y + 8 - k) % 8, rolled(trace_y[k], -16 * k), 0.0)
    trace_row[0] = packed
    along = [
        remote(trace_row.at[0], trace_row.at[k], tr_send.at[k], tr_recv.at[k], row[k - 1]) for k in range(1, 8)
    ]
    for copy in along:
        copy.start()

    for f in range(2):
        relay(*relays[f], "got")
        each_way(lambda i: halo(i, 0, f), 8, "start")

    for copy in spread_1[1:] + spread_2:
        copy.wait_recv()
    at = lane_iota((8, 128)) < 128 - off
    turn_back = lax.rem(128 - off, 128)
    for dz in range(2):
        for k in range(4):
            j = ((sx + 4 - k) % 4) * 2 + (sz + dz) % 2
            for plane in range(4):
                low = pltpu.roll(pieces[dz * 4 + k, plane], turn_back, 1)
                high = pltpu.roll(pieces[dz * 4 + k, 4 + plane], turn_back, 1)
                courant[plane, pl.ds(pl.multiple_of(j * 8, 8), 8)] = jnp.where(at, low, high)
    relay(*relays[4], "start")
    relay(*relays[3], "start")

    for copy in along:
        copy.wait_recv()
    own = jnp.zeros((16, 128), jnp.float32)
    for k in range(8):
        own = own + jnp.where((lane // 2) % 8 == (g + 8 - k) % 8, rolled(trace_row[k], -2 * k), 0.0)
    slots[...] = own

    def hand_out(group, x_index, at_place, wanted, action):
        for k in range(4):
            zk = (z + k) % 4
            src, dst = slots, tables.at[at_place]
            copy = remote(src, dst, table_send.at[group, k], table_recv.at[at_place], (s, block(x_index, zk)))
            mine = jnp.logical_and(x_index == xb, zk == z)

            @pl.when(jnp.logical_and(wanted, jnp.logical_not(mine)))
            def _():
                if action == "start":
                    copy.start()
                else:
                    copy.wait_send()

            if action == "start":
                @pl.when(jnp.logical_and(wanted, mine))
                def _():
                    pltpu.make_async_copy(src, dst, table_recv.at[at_place]).start()

    hands = (
        (0, home, 1 + place, home >= 0),
        (1, home + 1, 0, jnp.logical_and(place == 3, home < 15)),
        (2, home - 1, 5, jnp.logical_and(place == 0, home > 0)),
    )
    for hand in hands:
        hand_out(*hand, "start")

    for plane in range(16):
        image[plane] = jnp.zeros((16, 128), jnp.float32)

    relay(*relays[2], "got")
    each_way(lambda i: side(i, 0), 4, "start")
    relay(*relays[4], "got")
    each_way(lambda i: side(i, 2), 4, "start")

    for i in range(6):
        exists = {0: xb > 0, 5: xb < 15}.get(i, xb >= 0)

        @pl.when(exists)
        def _():
            remote(
                tables.at[i], tables.at[i], table_send.at[0, 0], table_recv.at[i], (s, d)
            ).wait_recv()

    for i in range(6):
        cell = tables[i, 8:9].astype(jnp.int32)
        near = ((cell >> 7) & 63) - (16 * z - 8)
        spot = jnp.where(jnp.logical_and(near >= 0, near < 32), (cell >> 13) * 32 + near, -1)
        onehot[i] = (
            lax.broadcasted_iota(jnp.int32, (128, 128), 0) == jnp.broadcast_to(spot, (128, 128))
        ).astype(jnp.float32).astype(jnp.bfloat16)
    relay(*relays[3], "got")
    each_way(lambda i: side(i, 1), 4, "start")
    each_way(lambda i: side(i, 0), 4, "got")
    each_way(lambda i: side(i, 2), 4, "got")
    each_way(lambda i: side(i, 0), 4, "sent")

    dims = (((1,), (1,)), ((), ()))

    def injection(t, kept, places):
        for i in places:
            value = tables[i, pl.ds(t, 1)]
            cell_lane = tables[i, 8:9].astype(jnp.int32) & 127
            hit = lax.broadcasted_iota(jnp.int32, (128, 128), 0) == jnp.broadcast_to(cell_lane, (128, 128))
            put = jnp.where(hit, jnp.broadcast_to(value, (128, 128)), 0.0)
            high = put.astype(jnp.bfloat16)
            low = (put - high.astype(jnp.float32)).astype(jnp.bfloat16)
            inj[kept, 128 * i : 128 * i + 128] = lax.dot_general(
                onehot[i], high, dims, preferred_element_type=jnp.float32
            ) + lax.dot_general(onehot[i], low, dims, preferred_element_type=jnp.float32)

    def step_wide(par, f):
        for quad in (0, 5):
            for i in range(4):
                plane = 4 + 4 * quad + i
                center, total = laplace(n.at[par, f], plane, 16, 16)
                following = 2.0 * center - m[f, plane, OWN_ROWS] + cc[4 * quad + i, 8:24] * total
                if f == 1:
                    following = following + inj[0, 128 * quad + 32 * i + 8 : 128 * quad + 32 * i + 24]
                m[f, plane, OWN_ROWS] = following

        @pl.loop(1, 5)
        def _(quad):
            for i in range(4):
                plane = 4 + 4 * quad + i
                center, total = laplace(n.at[par, f], plane, 8, 32)
                following = 2.0 * center - m[f, plane, ALL_ROWS] + cc[4 * quad + i] * total
                if f == 0:
                    image[plane - 8] += n[par, 1, plane, OWN_ROWS] * total[8:24]
                else:
                    following = following + inj[0, pl.ds(pl.multiple_of(128 * quad + 32 * i, 32), 32)]
                    image[plane - 8] += following[8:24] * lap[plane - 8]
                m[f, plane, ALL_ROWS] = following

    def step_own(par, f):
        @pl.loop(0, 4)
        def _(quad):
            for i in range(4):
                plane = 8 + 4 * quad + i
                center, total = laplace(m.at[f], plane, 16, 16)
                following = 2.0 * center - n[par, f, plane, OWN_ROWS] + cc[4 + 4 * quad + i, 8:24] * total
                if f == 0:
                    lap[plane - 8] = total
                else:
                    following = following + inj[1, pl.ds(pl.multiple_of(128 + 128 * quad + 32 * i + 8, 8), 16)]
                n[1 - par, f, plane, OWN_ROWS] = following

    def give_back(f, action):
        for i in range(4):
            src = n.at[0, f, pl.ds(8 + 4 * i, 4), OWN_ROWS]
            dst = outv.at[f, :, pl.ds(pl.multiple_of(16 * z, 16), 16)]
            copy = remote(src, dst, o_send.at[f, i], o_recv.at[f, z], (s, y * 8 + 4 * c + i))
            mine = g == 4 * c + i

            @pl.when(jnp.logical_not(mine))
            def _():
                if action == "start":
                    copy.start()
                else:
                    copy.wait_send()

            if action == "start":
                @pl.when(mine)
                def _():
                    pltpu.make_async_copy(src, dst, o_recv.at[f, z]).start()

    def turn_image():
        for plane in range(16):
            lap[plane] = pltpu.roll(image[plane] * (1.0 / STEPS), lax.rem(off, 128), 1)

    def send_gradient(action):
        for half in range(2):
            for i in range(4):
                src = lap.at[pl.ds(4 * i, 4), pl.ds(8 * half, 8)]
                dst = grads.at[s]
                to = (2 * z + half, y * 8 + 4 * c + i)
                copy = remote(src, dst, g_send.at[4 * half + i], g_recv.at[s], to)
                mine = jnp.logical_and(s == to[0], d == to[1])

                @pl.when(jnp.logical_not(mine))
                def _():
                    if action == "start":
                        copy.start()
                    else:
                        copy.wait_send()

                if action == "start":
                    @pl.when(mine)
                    def _():
                        pltpu.make_async_copy(src, dst, g_recv.at[s]).start()

    blocks = STEPS // 2

    @pl.loop(0, blocks)
    def _(b):
        par = b % 2
        for f in range(2):
            if f == 1:
                injection(2 * b, 0, range(6))
                injection(2 * b + 1, 1, range(1, 5))

                @pl.when(b == 0)
                def _():
                    each_way(lambda i: side(i, 1), 4, "got")
                    each_way(lambda i: side(i, 1), 4, "sent")

            each_way(lambda i: halo(i, par, f), 8, "got")
            step_wide(par, f)

            @pl.when(b > 0)
            def _():
                each_way(lambda i: halo(i, 1 - par, f), 8, "sent")

            if f == 1:
                @pl.when(b == blocks - 1)
                def _():
                    turn_image()
                    send_gradient("start")

            step_own(par, f)

            @pl.when(b < blocks - 1)
            def _():
                each_way(lambda i: halo(i, 1 - par, f), 8, "start")

            if f == 0:
                @pl.when(b == blocks - 1)
                def _():
                    give_back(0, "start")

    give_back(1, "start")
    results = [
        pltpu.make_async_copy(outv.at[f], ref.at[0], small_sem.at[f]) for f, ref in enumerate((src_out, adj_out))
    ]
    for f in range(2):
        for k in range(4):
            got = outv.at[f, :, pl.ds(16 * k, 16)]
            remote(got, got, o_send.at[f, k], o_recv.at[f, k], (s, d)).wait_recv()
        results[f].start()
    for j in range(8):
        remote(grads.at[j], grads.at[j], g_send.at[j], g_recv.at[j], (s, d)).wait_recv()
    lane8 = lane_iota((8, 128)).astype(jnp.float32)
    for plane in range(4):
        low = jnp.zeros((8, 128), jnp.float32)
        high = jnp.zeros((8, 128), jnp.float32)
        for dz in range(2):
            for k in range(4):
                j = ((sx + 4 - k) % 4) * 2 + (sz + dz) % 2
                part = grads[j, plane]
                start = pieces[dz * 4 + k, 8]
                low = low + jnp.where(lane8 >= start, part, 0.0)
                high = high + jnp.where(lane8 < start, part, 0.0)
        summed[plane, :, 0:128] = low
        summed[plane, :, 128:256] = high
    gradient = pltpu.make_async_copy(summed, grad_out, small_sem.at[2])
    gradient.start()
    for copy in first + along + spread_1 + spread_2:
        copy.wait_send()
    for args in relays:
        relay(*args, "sent")
    for hand in hands:
        hand_out(*hand, "sent")
    each_way(lambda i: side(i, 2), 4, "sent")
    for f in range(2):
        each_way(lambda i: halo(i, 1, f), 8, "sent")
        give_back(f, "sent")
    send_gradient("sent")
    for copy in results + [gradient]:
        copy.wait()


def deliver(*refs):
    given, wanted, held, sems = refs[0:3], refs[3:6], refs[6:9], refs[9]
    into = [pltpu.make_async_copy(a, b, sems.at[0, i]) for i, (a, b) in enumerate(zip(given, held, strict=True))]
    out = [pltpu.make_async_copy(a, b, sems.at[1, i]) for i, (a, b) in enumerate(zip(held, wanted, strict=True))]
    for copy in into:
        copy.start()
    for i in range(3):
        into[i].wait()
        out[i].start()
    for copy in out:
        copy.wait()


def shards(source_prev, source_now, adjoint_prev, adjoint_now, squared_courant, offsets, traces, receiver_cells, counts):
    field = jax.ShapeDtypeStruct(source_now.shape, jnp.float32)
    hbm = pl.BlockSpec(memory_space=pltpu.HBM)
    f32 = jnp.float32
    dma = pltpu.SemaphoreType.DMA
    results = pl.pallas_call(
        kernel,
        out_shape=(field, field, jax.ShapeDtypeStruct(squared_courant.shape, f32)),
        in_specs=[hbm] * 9,
        out_specs=(hbm, hbm, hbm),
        scratch_shapes=[
            pltpu.VMEM((2, 2, 32, 48, 128), f32),
            pltpu.VMEM((2, 32, 48, 128), f32),
            pltpu.VMEM((24, 32, 128), f32),
            pltpu.VMEM((4, 64, 128), f32),
            pltpu.VMEM((16, 16, 128), f32),
            pltpu.VMEM((16, 16, 128), f32),
            pltpu.VMEM((2, 768, 128), f32),
            pltpu.VMEM((8, 9, 8, 128), f32),
            pltpu.VMEM((8, 4, 8, 128), f32),
            pltpu.VMEM((16, 128), f32),
            pltpu.VMEM((8, 16, 128), f32),
            pltpu.VMEM((8, 16, 128), f32),
            pltpu.VMEM((16, 128), f32),
            pltpu.VMEM((6, 16, 128), f32),
            pltpu.VMEM((6, 128, 128), jnp.bfloat16),
            pltpu.VMEM((8, 128), f32),
            pltpu.VMEM((1, 128), jnp.int32),
            pltpu.VMEM((1, 64), jnp.int32),
            pltpu.SMEM((1,), jnp.int32),
            pltpu.VMEM((4, 8, 256), f32),
            pltpu.VMEM((2, 4, 64, 128), f32),
            dma((6,)),
            dma((5, 4)), dma((5, 4)),
            dma((3, 4)), dma((6,)),
            dma((2, 2, 8)), dma((2, 2, 8)),
            dma((3, 4)), dma((3, 4)),
            dma((8,)), dma((8,)), dma((8,)), dma((8,)), dma((8,)), dma((8,)), dma((8,)), dma((8,)),
            dma((2, 4)), dma((2, 4)),
        ],
        compiler_params=pltpu.CompilerParams(
            collective_id=0, has_side_effects=True, vmem_limit_bytes=60 * 1024 * 1024
        ),
    )(source_prev, source_now, adjoint_prev, adjoint_now, squared_courant, offsets, traces, receiver_cells, counts)
    return pl.pallas_call(
        deliver,
        out_shape=tuple(jax.ShapeDtypeStruct(r.shape, f32) for r in results),
        in_specs=[hbm] * 3,
        out_specs=(hbm,) * 3,
        scratch_shapes=[pltpu.VMEM(r.shape, f32) for r in results] + [dma((2, 3))],
        compiler_params=pltpu.CompilerParams(vmem_limit_bytes=60 * 1024 * 1024),
    )(*results)


def solution(mesh):
    placed = (
        P("shot", "dom", None, None),
        P("shot", "dom", None, None),
        P("shot", "dom", None, None),
        P("shot", "dom", None, None),
        P("dom", "shot", None),
        P("shot"),
        P("shot", None, "dom"),
        P("shot", None, "dom"),
        P("shot", "dom", None),
    )
    return jax.shard_map(
        shards,
        mesh=mesh,
        in_specs=placed,
        out_specs=(
            P("shot", "dom", None, None),
            P("shot", "dom", None, None),
            P("dom", "shot", None),
        ),
        check_vma=False,
    )
```

time: 79.9 us -> 76.3 us (0.955)
  the two profiles are of different devices: /device:TPU:33 before, /device:TPU:25 now
where the time goes in v3:
time: 76.3 us; the launch traced here: 76.1 us
  Pallas kernels  74.8 us (98%)
  between operations  1.29 us (2%)
    pallas_call x1, Pallas kernels, shards(): pl.pallas_call(kernel, out_shape=(field, field, jax.ShapeDtypeStruct(squa...  73.1 us
    pallas_call x1, Pallas kernels, shards(): pl.pallas_call(deliver, out_shape=tuple((jax.ShapeDtypeStruct(r.shape, f3...  1.68 us

profile of v3, /device:TPU:25, one launch (start us, length us, event | category | flops | bytes accessed | tf_op | source)
XLA Modules:
  0.0 76.1 jit_solution(5797151044714158755)
XLA Ops:
  1.3 73.1 %shard_map.112 = (f32[1,4,64,128]{3,2,1,0:T(8,128)}, f32[1,4,64,128]{3,2,1,0:T(8,128)}, f32[4,8,256]{2,1,0:T(8,128)}) custom-call(f32[1,4,64,128]{3,2,1,0:T(8,128)} %src_prev.1, f32[1,4,64,128]{3,2,1,0:T(8,128)} %src_now.1, f32[1,4,64,128]{3,2,1,0:T(8,128)} %adj_prev.1, f32[1,4,64,128]{3,2,1,0:T(8,128)} %adj_now.1, f32[4,8,256]{2,1,0:T(8,128)} %model_in.1, ...), custom_call_target="tpu_custom_call" | custom-call | tf_op jit(solution)/shard_map/pallas_call | solution.py:545
  74.4 1.7 %shard_map.113 = (f32[1,4,64,128]{3,2,1,0:T(8,128)}, f32[1,4,64,128]{3,2,1,0:T(8,128)}, f32[4,8,256]{2,1,0:T(8,128)}) custom-call(f32[1,4,64,128]{3,2,1,0:T(8,128)} %get-tuple-element.6.refs_0_, f32[1,4,64,128]{3,2,1,0:T(8,128)} %get-tuple-element.7.refs_1_, f32[4,8,256]{2,1,0:T(8,128)} %get-tuple-element.8.refs_2_), custom_call_target="tpu_custom_call" | custom-call | tf_op jit(solution)/shard_map/pallas_call | solution.py:584

commit v4 on v3

--- a/solution.py
+++ b/solution.py
@@ -27,15 +27,18 @@
     return pltpu.roll(value, shift % 128, value.ndim - 1) if shift % 128 else value
 
 
-def laplace(ref, plane, first, rows):
+def along_lanes(value, band):
+    high = value.astype(jnp.bfloat16)
+    low = (value - high.astype(jnp.float32)).astype(jnp.bfloat16)
+    return jnp.dot(jnp.concatenate([high, low, high], 1), band[...], preferred_element_type=jnp.float32)
+
+
+def laplace(ref, plane, first, rows, along):
     center = ref[plane, pl.ds(first, rows)]
-    lanes = lane_iota((rows, 128))
-    total = 3.0 * COEFFS[0] * center
+    total = 3.0 * COEFFS[0] * center + along
     for reach in range(1, 5):
         pair = ref[plane + reach, pl.ds(first, rows)] + ref[plane - reach, pl.ds(first, rows)]
         pair = pair + ref[plane, pl.ds(first + reach, rows)] + ref[plane, pl.ds(first - reach, rows)]
-        pair = pair + jnp.where(lanes >= reach, rolled(center, reach), 0.0)
-        pair = pair + jnp.where(lanes < 128 - reach, rolled(center, -reach), 0.0)
         total = total + COEFFS[reach] * pair
     return center, total
 
@@ -44,9 +47,9 @@
     src_prev, src_now, adj_prev, adj_now, model_in, offsets_in, traces_in, cells_in, counts_in,
     src_out, adj_out, grad_out,
     n, m, cc, courant, image, lap, inj, pieces, grads, trace_send, trace_y, trace_row, slots, tables, onehot,
-    traces, cells, counts, offsets, summed, outv,
+    traces, cells, counts, offsets, summed, outv, band, third, offs,
     small_sem, relay_send, relay_recv, table_send, table_recv, halo_send, halo_recv, side_send, side_recv,
-    ty_send, ty_recv, tr_send, tr_recv, c_send, c_recv, g_send, g_recv, o_send, o_recv,
+    ty_send, ty_recv, tr_send, tr_recv, c_send, c_recv, cr_send, cr_recv, f_send, f_recv, g_send, g_recv, o_send, o_recv,
 ):
     s = lax.axis_index("shot")
     d = lax.axis_index("dom")
@@ -135,20 +138,23 @@
             def _():
                 greet((s, y * 8 + 2 * sx + hc))
 
-    expected = 21 + 4 * beyond.astype(jnp.int32) + 8 - own_gradient.astype(jnp.int32)
+    for i in range(4):
+        greet((2 * sx + 1 - sz, y * 8 + 4 * c + i))
+    expected = 25 + 4 * beyond.astype(jnp.int32) + 8 - own_gradient.astype(jnp.int32)
     for copy in small:
         copy.wait()
     off = offsets[0]
-    pieces[0, 8] = jnp.full((8, 128), off, jnp.int32).astype(jnp.float32)
+    offs[0] = jnp.full((8, 128), off, jnp.int32).astype(jnp.float32)
     for copy in halves:
         copy.wait()
     pl.semaphore_wait(barrier, expected)
 
-    spread_1 = [
-        remote(pieces.at[0], pieces.at[dz * 4 + k], c_send.at[dz * 4 + k], c_recv.at[dz * 4 + k], shot[dz, k])
-        for dz, k in ((1, 0), (0, 1), (0, 2), (0, 3))
+    spread_1 = [remote(pieces.at[0], pieces.at[k], c_send.at[k], c_recv.at[k], shot[0, k]) for k in range(1, 4)]
+    told = [
+        remote(offs.at[0], offs.at[dz * 4 + k], f_send.at[dz * 4 + k], f_recv.at[dz * 4 + k], shot[dz, k])
+        for dz, k in others
     ]
-    for copy in spread_1:
+    for copy in spread_1 + told:
         copy.start()
 
     def relay(array, source, target, base, rows, action):
@@ -183,7 +189,6 @@
         (1, adj_now.at[0], n.at[0, 1], 8, OWN_ROWS),
         (2, src_prev.at[0], m.at[0], 8, OWN_ROWS),
         (3, adj_prev.at[0], m.at[1], 8, OWN_ROWS),
-        (4, courant, cc, 4, pl.ds(8, 16)),
     )
     relay(*relays[0], "start")
     relay(*relays[1], "start")
@@ -233,6 +238,15 @@
                         make(i).start()
                     else:
                         make(i).wait_send()
+
+    apart = jnp.abs(lax.broadcasted_iota(jnp.int32, (128, 128), 0) - lane_iota((128, 128)))
+    weights = jnp.zeros((128, 128), jnp.float32)
+    for reach in range(1, 5):
+        weights = jnp.where(apart == reach, COEFFS[reach], weights)
+    weights_high = weights.astype(jnp.bfloat16)
+    band[0:128] = weights_high
+    band[128:256] = weights_high
+    band[256:384] = (weights - weights_high.astype(jnp.float32)).astype(jnp.bfloat16)
 
     spread = (lax.broadcasted_iota(jnp.int32, (64, 128), 0) == lane_iota((64, 128)) // 2).astype(jnp.float32)
     filled = jnp.broadcast_to(counts[...].astype(jnp.float32), (8, 64))
@@ -249,12 +263,52 @@
     relay(*relays[2], "start")
     trace_y[0] = trace_send[...]
 
-    spread_1[0].wait_recv()
-    spread_2 = [
-        remote(pieces.at[4], pieces.at[4 + k], c_send.at[4 + k], c_recv.at[4 + k], shot[0, k]) for k in range(1, 4)
-    ]
-    for copy in spread_2:
-        copy.start()
+    for copy in spread_1:
+        copy.wait_recv()
+    for copy in told:
+        copy.wait_recv()
+
+    def window(target, tile, shift):
+        at = lane_iota((8, 128)).astype(jnp.float32) < 128.0 - tile
+        turn_back = lax.rem(128 - shift, 128)
+        for k in range(4):
+            for plane in range(4):
+                low = pltpu.roll(pieces[k, plane], turn_back, 1)
+                high = pltpu.roll(pieces[k, 4 + plane], turn_back, 1)
+                courant[target, k, plane] = jnp.where(at, low, high)
+
+    def hand_model(target, action):
+        for k in range(4):
+            rows_at = (sx + 4 - k) % 4
+            src = courant.at[target, k]
+            dst = cc.at[pl.ds(4 + 4 * place, 4), pl.ds(pl.multiple_of(8 + 8 * sz, 8), 8)]
+            where = ((s, 2 * sx + 1 - sz)[target], y * 8 + 2 * rows_at + hc)
+            copy = remote(src, dst, cr_send.at[target, k], cr_recv.at[place, sz], where)
+            mine = jnp.logical_and(stays, rows_at == z)
+            if target:
+                if action == "start":
+                    copy.start()
+                else:
+                    copy.wait_send()
+                continue
+
+            @pl.when(jnp.logical_not(mine))
+            def _():
+                if action == "start":
+                    copy.start()
+                else:
+                    copy.wait_send()
+
+            if action == "start":
+                @pl.when(mine)
+                def _():
+                    pltpu.make_async_copy(src, dst, cr_recv.at[place, sz]).start()
+
+    window(1, offs[4], jnp.max(offs[4]).astype(jnp.int32))
+    hand_model(1, "start")
+    window(0, offs[0], off)
+    hand_model(0, "start")
+
     for copy in first:
         copy.wait_recv()
     lane = lane_iota((16, 128))
@@ -272,18 +326,6 @@
         relay(*relays[f], "got")
         each_way(lambda i: halo(i, 0, f), 8, "start")
 
-    for copy in spread_1[1:] + spread_2:
-        copy.wait_recv()
-    at = lane_iota((8, 128)) < 128 - off
-    turn_back = lax.rem(128 - off, 128)
-    for dz in range(2):
-        for k in range(4):
-            j = ((sx + 4 - k) % 4) * 2 + (sz + dz) % 2
-            for plane in range(4):
-                low = pltpu.roll(pieces[dz * 4 + k, plane], turn_back, 1)
-                high = pltpu.roll(pieces[dz * 4 + k, 4 + plane], turn_back, 1)
-                courant[plane, pl.ds(pl.multiple_of(j * 8, 8), 8)] = jnp.where(at, low, high)
-    relay(*relays[4], "start")
     relay(*relays[3], "start")
 
     for copy in along:
@@ -325,7 +367,10 @@
 
     relay(*relays[2], "got")
     each_way(lambda i: side(i, 0), 4, "start")
-    relay(*relays[4], "got")
+    for p in range(4):
+        for half in range(2):
+            got = cc.at[pl.ds(4 + 4 * p, 4), pl.ds(8 + 8 * half, 8)]
+            remote(got, got, cr_send.at[half, p], cr_recv.at[p, half], (s, d)).wait_recv()
     each_way(lambda i: side(i, 2), 4, "start")
 
     for i in range(6):
@@ -365,10 +410,16 @@
             ) + lax.dot_general(onehot[i], low, dims, preferred_element_type=jnp.float32)
 
     def step_wide(par, f):
+        for quad in range(6):
+            if quad in (0, 5):
+                rows, where = OWN_ROWS, pl.ds(128 * quad, 64)
+            else:
+                rows, where = ALL_ROWS, pl.ds(128 * quad, 128)
+            third[where] = along_lanes(n[par, f, pl.ds(4 + 4 * quad, 4), rows].reshape(where.size, 128), band)
         for quad in (0, 5):
             for i in range(4):
                 plane = 4 + 4 * quad + i
-                center, total = laplace(n.at[par, f], plane, 16, 16)
+                center, total = laplace(n.at[par, f], plane, 16, 16, third[128 * quad + 16 * i : 128 * quad + 16 * i + 16])
                 following = 2.0 * center - m[f, plane, OWN_ROWS] + cc[4 * quad + i, 8:24] * total
                 if f == 1:
                     following = following + inj[0, 128 * quad + 32 * i + 8 : 128 * quad + 32 * i + 24]
@@ -378,7 +429,8 @@
         def _(quad):
             for i in range(4):
                 plane = 4 + 4 * quad + i
-                center, total = laplace(n.at[par, f], plane, 8, 32)
+                along = third[pl.ds(pl.multiple_of(128 * quad + 32 * i, 32), 32)]
+                center, total = laplace(n.at[par, f], plane, 8, 32, along)
                 following = 2.0 * center - m[f, plane, ALL_ROWS] + cc[4 * quad + i] * total
                 if f == 0:
                     image[plane - 8] += n[par, 1, plane, OWN_ROWS] * total[8:24]
@@ -388,11 +440,15 @@
                 m[f, plane, ALL_ROWS] = following
 
     def step_own(par, f):
+        for quad in range(4):
+            third[pl.ds(64 * quad, 64)] = along_lanes(m[f, pl.ds(8 + 4 * quad, 4), OWN_ROWS].reshape(64, 128), band)
+
         @pl.loop(0, 4)
         def _(quad):
             for i in range(4):
                 plane = 8 + 4 * quad + i
-                center, total = laplace(m.at[f], plane, 16, 16)
+                along = third[pl.ds(pl.multiple_of(64 * quad + 16 * i, 16), 16)]
+                center, total = laplace(m.at[f], plane, 16, 16, along)
                 following = 2.0 * center - n[par, f, plane, OWN_ROWS] + cc[4 + 4 * quad + i, 8:24] * total
                 if f == 0:
                     lap[plane - 8] = total
@@ -502,15 +558,17 @@
             for k in range(4):
                 j = ((sx + 4 - k) % 4) * 2 + (sz + dz) % 2
                 part = grads[j, plane]
-                start = pieces[dz * 4 + k, 8]
+                start = offs[dz * 4 + k]
                 low = low + jnp.where(lane8 >= start, part, 0.0)
                 high = high + jnp.where(lane8 < start, part, 0.0)
         summed[plane, :, 0:128] = low
         summed[plane, :, 128:256] = high
     gradient = pltpu.make_async_copy(summed, grad_out, small_sem.at[2])
     gradient.start()
-    for copy in first + along + spread_1 + spread_2:
+    for copy in first + along + spread_1 + told:
         copy.wait_send()
+    for target in range(2):
+        hand_model(target, "sent")
     for args in relays:
         relay(*args, "sent")
     for hand in hands:
@@ -551,11 +609,11 @@
             pltpu.VMEM((2, 2, 32, 48, 128), f32),
             pltpu.VMEM((2, 32, 48, 128), f32),
             pltpu.VMEM((24, 32, 128), f32),
-            pltpu.VMEM((4, 64, 128), f32),
+            pltpu.VMEM((2, 4, 4, 8, 128), f32),
             pltpu.VMEM((16, 16, 128), f32),
             pltpu.VMEM((16, 16, 128), f32),
             pltpu.VMEM((2, 768, 128), f32),
-            pltpu.VMEM((8, 9, 8, 128), f32),
+            pltpu.VMEM((4, 8, 8, 128), f32),
             pltpu.VMEM((8, 4, 8, 128), f32),
             pltpu.VMEM((16, 128), f32),
             pltpu.VMEM((8, 16, 128), f32),
@@ -569,12 +627,16 @@
             pltpu.SMEM((1,), jnp.int32),
             pltpu.VMEM((4, 8, 256), f32),
             pltpu.VMEM((2, 4, 64, 128), f32),
+            pltpu.VMEM((384, 128), jnp.bfloat16),
+            pltpu.VMEM((768, 128), f32),
+            pltpu.VMEM((8, 8, 128), f32),
             dma((6,)),
-            dma((5, 4)), dma((5, 4)),
+            dma((4, 4)), dma((4, 4)),
             dma((3, 4)), dma((6,)),
             dma((2, 2, 8)), dma((2, 2, 8)),
             dma((3, 4)), dma((3, 4)),
-            dma((8,)), dma((8,)), dma((8,)), dma((8,)), dma((8,)), dma((8,)), dma((8,)), dma((8,)),
+            dma((8,)), dma((8,)), dma((8,)), dma((8,)), dma((4,)), dma((4,)), dma((2, 4)), dma((4, 2)),
+            dma((8,)), dma((8,)), dma((8,)), dma((8,)),
             dma((2, 4)), dma((2, 4)),
         ],
         compiler_params=pltpu.CompilerParams(

time: 76.3 us -> 73.6 us (0.965)
  Pallas kernels: 74.8 us -> 72.1 us
    pallas_call x1, Pallas kernels: 73.1 us -> 70.4 us  [shards(): pl.pallas_call(kernel, out_shape=(field, field, jax.ShapeDtypeStruct(squa...]
where the time goes in v4:
time: 73.6 us; the launch traced here: 73.4 us
  Pallas kernels  72.1 us (98%)
  between operations  1.29 us (2%)
    pallas_call x1, Pallas kernels, shards(): pl.pallas_call(kernel, out_shape=(field, field, jax.ShapeDtypeStruct(squa...  70.4 us
    pallas_call x1, Pallas kernels, shards(): pl.pallas_call(deliver, out_shape=tuple((jax.ShapeDtypeStruct(r.shape, f3...  1.68 us

profile of v4, /device:TPU:25, one launch (start us, length us, event | category | flops | bytes accessed | tf_op | source)
XLA Modules:
  0.0 73.4 jit_solution(4599553330854902728)
XLA Ops:
  1.3 70.4 %shard_map.112 = (f32[1,4,64,128]{3,2,1,0:T(8,128)}, f32[1,4,64,128]{3,2,1,0:T(8,128)}, f32[4,8,256]{2,1,0:T(8,128)}) custom-call(f32[1,4,64,128]{3,2,1,0:T(8,128)} %src_prev.1, f32[1,4,64,128]{3,2,1,0:T(8,128)} %src_now.1, f32[1,4,64,128]{3,2,1,0:T(8,128)} %adj_prev.1, f32[1,4,64,128]{3,2,1,0:T(8,128)} %adj_now.1, f32[4,8,256]{2,1,0:T(8,128)} %model_in.1, ...), custom_call_target="tpu_custom_call" | custom-call | tf_op jit(solution)/shard_map/pallas_call | solution.py:603
  71.7 1.7 %shard_map.113 = (f32[1,4,64,128]{3,2,1,0:T(8,128)}, f32[1,4,64,128]{3,2,1,0:T(8,128)}, f32[4,8,256]{2,1,0:T(8,128)}) custom-call(f32[1,4,64,128]{3,2,1,0:T(8,128)} %get-tuple-element.6.refs_0_, f32[1,4,64,128]{3,2,1,0:T(8,128)} %get-tuple-element.7.refs_1_, f32[4,8,256]{2,1,0:T(8,128)} %get-tuple-element.8.refs_2_), custom_call_target="tpu_custom_call" | custom-call | tf_op jit(solution)/shard_map/pallas_call | solution.py:646

commit v5 on v4

--- a/solution.py
+++ b/solution.py
@@ -439,7 +439,25 @@
                     image[plane - 8] += following[8:24] * lap[plane - 8]
                 m[f, plane, ALL_ROWS] = following
 
-    def step_own(par, f):
+    def give_part(f, i, action):
+        src = n.at[0, f, pl.ds(8 + 4 * i, 4), OWN_ROWS]
+        dst = outv.at[f, :, pl.ds(pl.multiple_of(16 * z, 16), 16)]
+        copy = remote(src, dst, o_send.at[f, i], o_recv.at[f, z], (s, y * 8 + 4 * c + i))
+        mine = g == 4 * c + i
+
+        @pl.when(jnp.logical_not(mine))
+        def _():
+            if action == "start":
+                copy.start()
+            else:
+                copy.wait_send()
+
+        if action == "start":
+            @pl.when(mine)
+            def _():
+                pltpu.make_async_copy(src, dst, o_recv.at[f, z]).start()
+
+    def step_own(par, f, last):
         for quad in range(4):
             third[pl.ds(64 * quad, 64)] = along_lanes(m[f, pl.ds(8 + 4 * quad, 4), OWN_ROWS].reshape(64, 128), band)
 
@@ -456,24 +474,9 @@
                     following = following + inj[1, pl.ds(pl.multiple_of(128 + 128 * quad + 32 * i + 8, 8), 16)]
                 n[1 - par, f, plane, OWN_ROWS] = following
 
-    def give_back(f, action):
-        for i in range(4):
-            src = n.at[0, f, pl.ds(8 + 4 * i, 4), OWN_ROWS]
-            dst = outv.at[f, :, pl.ds(pl.multiple_of(16 * z, 16), 16)]
-            copy = remote(src, dst, o_send.at[f, i], o_recv.at[f, z], (s, y * 8 + 4 * c + i))
-            mine = g == 4 * c + i
-
-            @pl.when(jnp.logical_not(mine))
+            @pl.when(last)
             def _():
-                if action == "start":
-                    copy.start()
-                else:
-                    copy.wait_send()
-
-            if action == "start":
-                @pl.when(mine)
-                def _():
-                    pltpu.make_async_copy(src, dst, o_recv.at[f, z]).start()
+                give_part(f, quad, "start")
 
     def turn_image():
         for plane in range(16):
@@ -528,18 +531,13 @@
                     turn_image()
                     send_gradient("start")
 
-            step_own(par, f)
+            step_own(par, f, b == blocks - 1)
 
             @pl.when(b < blocks - 1)
             def _():
                 each_way(lambda i: halo(i, 1 - par, f), 8, "start")
 
-            if f == 0:
-                @pl.when(b == blocks - 1)
-                def _():
-                    give_back(0, "start")
-
-    give_back(1, "start")
+
     results = [
         pltpu.make_async_copy(outv.at[f], ref.at[0], small_sem.at[f]) for f, ref in enumerate((src_out, adj_out))
     ]
@@ -576,7 +574,8 @@
     each_way(lambda i: side(i, 2), 4, "sent")
     for f in range(2):
         each_way(lambda i: halo(i, 1, f), 8, "sent")
-        give_back(f, "sent")
+        for i in range(4):
+            give_part(f, i, "sent")
     send_gradient("sent")
     for copy in results + [gradient]:
         copy.wait()

time: 73.6 us -> 73.6 us (level)
  no operation moved by 1% of the time
where the time goes in v5:
time: 73.6 us; the launch traced here: 73.4 us
  Pallas kernels  72.1 us (98%)
  between operations  1.29 us (2%)
    pallas_call x1, Pallas kernels, shards(): pl.pallas_call(kernel, out_shape=(field, field, jax.ShapeDtypeStruct(squa...  70.4 us
    pallas_call x1, Pallas kernels, shards(): pl.pallas_call(deliver, out_shape=tuple((jax.ShapeDtypeStruct(r.shape, f3...  1.68 us

profile of v5, /device:TPU:25, one launch (start us, length us, event | category | flops | bytes accessed | tf_op | source)
XLA Modules:
  0.0 73.4 jit_solution(12167002348577370221)
XLA Ops:
  1.3 70.4 %shard_map.112 = (f32[1,4,64,128]{3,2,1,0:T(8,128)}, f32[1,4,64,128]{3,2,1,0:T(8,128)}, f32[4,8,256]{2,1,0:T(8,128)}) custom-call(f32[1,4,64,128]{3,2,1,0:T(8,128)} %src_prev.1, f32[1,4,64,128]{3,2,1,0:T(8,128)} %src_now.1, f32[1,4,64,128]{3,2,1,0:T(8,128)} %adj_prev.1, f32[1,4,64,128]{3,2,1,0:T(8,128)} %adj_now.1, f32[4,8,256]{2,1,0:T(8,128)} %model_in.1, ...), custom_call_target="tpu_custom_call" | custom-call | tf_op jit(solution)/shard_map/pallas_call | solution.py:602
  71.7 1.7 %shard_map.113 = (f32[1,4,64,128]{3,2,1,0:T(8,128)}, f32[1,4,64,128]{3,2,1,0:T(8,128)}, f32[4,8,256]{2,1,0:T(8,128)}) custom-call(f32[1,4,64,128]{3,2,1,0:T(8,128)} %get-tuple-element.6.refs_0_, f32[1,4,64,128]{3,2,1,0:T(8,128)} %get-tuple-element.7.refs_1_, f32[4,8,256]{2,1,0:T(8,128)} %get-tuple-element.8.refs_2_), custom_call_target="tpu_custom_call" | custom-call | tf_op jit(solution)/shard_map/pallas_call | solution.py:645
